TPU v7x, 128 devices: a whole 4x4x4 slice. The times are simulated.
128 devices in a mesh: blk: 16 (over x, z_lo, core), rows: 8 (over y, z_hi).
Axes of the slice: x: 4, y: 4, z: 4 (z_hi: 2, z_lo: 2; z = z_hi * 2 + z_lo), core: 2. Of those that a mesh axis runs over, the one named last changes fastest.
Arguments:
- points: float32 [196608, 256], P(('blk', 'rows')), may hold values from -6 to 6
- centres: float32 [8192, 256], P('blk'), may hold values from -6 to 6
- coefficients: float32 [8192], P('blk'), may hold values from -0.0625 to 0.0625
Outputs:
- normal_product: float32 [8192], P('blk')
All inputs are finite; a program needn't handle non-finite values.
Results may differ from a plain program's by a relative error of at most 0.0003.
Values sent between devices are 32-bit elements; how exact they have to be, the bound alone decides.
No kernel may reach another device: no remote copies, remote signals or barrier semaphores. Data moves between devices by JAX's collectives and lax.ppermute only.
A program may use at most 128 MiB of HBM per device.

v0:
```python
import math

import jax
import jax.numpy as jnp
from jax import lax
from jax.sharding import PartitionSpec as P


def passed_along(x, axis, by):
    peers = lax.axis_size(axis)
    return lax.ppermute(x, axis, [(i, (i + by) % peers) for i in range(peers)])


def kernel_block(points, point_sq, block):
    width = points.shape[1]
    inner = jnp.dot(
        points, block.T, precision=lax.Precision.HIGHEST, preferred_element_type=jnp.float32
    )
    block_sq = jnp.sum(block * block, axis=1)
    dist_sq = point_sq[:, None] + block_sq[None, :] - 2.0 * inner
    return jnp.exp((2.0 * width - dist_sq) * (0.5 / math.sqrt(width)))


def apply_block(points, point_sq, block, coef):
    kernel = kernel_block(points, point_sq, block)
    return jnp.dot(
        kernel, coef, precision=lax.Precision.HIGHEST, preferred_element_type=jnp.float32
    )


def transpose_block(points, point_sq, block, point_values):
    kernel = kernel_block(points, point_sq, block)
    return jnp.dot(
        point_values, kernel, precision=lax.Precision.HIGHEST, preferred_element_type=jnp.float32
    )


def body(points, centres, coefficients):
    cycle_size = lax.axis_size("blk")
    total_points = points.shape[0] * cycle_size * lax.axis_size("rows")
    point_sq = jnp.sum(points * points, axis=1)
    start = jnp.zeros((points.shape[0],), jnp.float32)

    def visit(step, carry):
        block, coef, values = carry
        values = values + apply_block(points, point_sq, block, coef)
        block, coef = passed_along((block, coef), "blk", 1)
        return (block, coef, values)

    block, coef, values = lax.fori_loop(0, cycle_size - 1, visit, (centres, coefficients, start))
    point_values = values + apply_block(points, point_sq, block, coef)

    def sweep_step(step, carry):
        block, running = carry
        running = running + transpose_block(points, point_sq, block, point_values)
        block, running = passed_along((block, running), "blk", 1)
        return (block, running)

    empty = jnp.zeros((centres.shape[0],), jnp.float32)
    block, running = lax.fori_loop(0, cycle_size - 1, sweep_step, (centres, empty))
    running = running + transpose_block(points, point_sq, block, point_values)
    owned = passed_along(running, "blk", 1)
    summed = lax.psum(owned, "rows")
    return summed / total_points


def solution(mesh):
    return jax.shard_map(
        body,
        mesh=mesh,
        in_specs=(P(("blk", "rows"), None), P("blk", None), P("blk")),
        out_specs=P("blk"),
        check_vma=False,
    )
```

profile of v0, /device:TPU:0, one launch (start us, length us, event | category | flops | bytes accessed | tf_op | source)
XLA Modules:
  0.0 406.1 jit_solution(4721653384029265826)
XLA Ops:
  3.8 193.8 %while.28 = (s32[]{:T(128)}, f32[512,256]{1,0:T(8,128)}, f32[512]{0:T(512)S(1)}, f32[1536]{0:T(1024)S(1)}, f32[1536]{0:T(1024)S(1)}, /*index=5*/f32[1536,256]{1,0:T(8,128)}, s32[]{:T(128)}, s32[]{:T(128)}) while((s32[]{:T(128)}, f32[512,256]{1,0:T(8,128)}, f32[512]{0:T(512)S(1)}, f32[1536]{0:T(1024)S(1)}, f32[1536]{0:T(1024)S(1)}, ...), condition=%wide.region_3.0_spmd.clone, body=%wide.region_1.0_spmd.clone.sunk | while | flops 2429553152 | bytes 12107951 | solution.py:50
  9.0 4.8 %fusion.57 = f32[1536,512]{1,0:T(8,128)S(1)} fusion(f32[1536,256]{1,0:T(8,128)} %get-tuple-element.247, f32[512,256]{1,0:T(8,128)} %copy.9, f32[512]{0:T(512)S(1)} %multiply_reduce_fusion.8, f32[1536]{0:T(1024)S(1)} %get-tuple-element.246), kind=kOutput, calls=%fused_computation.10.clone.1 | convolution fusion | flops 2419851264 | bytes 5251072 | tf_op jit(solution)/shard_map/while/body/eval_jaxpr/dot_general | solution.py:16
  58.5 4.8 %fusion.57 = f32[1536,512]{1,0:T(8,128)S(1)} fusion(f32[1536,256]{1,0:T(8,128)} %get-tuple-element.247, f32[512,256]{1,0:T(8,128)} %copy.9, f32[512]{0:T(512)S(1)} %multiply_reduce_fusion.8, f32[1536]{0:T(1024)S(1)} %get-tuple-element.246), kind=kOutput, calls=%fused_computation.10.clone.1 | convolution fusion | flops 2419851264 | bytes 5251072 | tf_op jit(solution)/shard_map/while/body/eval_jaxpr/dot_general | solution.py:16
  110.2 4.8 %fusion.57 = f32[1536,512]{1,0:T(8,128)S(1)} fusion(f32[1536,256]{1,0:T(8,128)} %get-tuple-element.247, f32[512,256]{1,0:T(8,128)} %copy.9, f32[512]{0:T(512)S(1)} %multiply_reduce_fusion.8, f32[1536]{0:T(1024)S(1)} %get-tuple-element.246), kind=kOutput, calls=%fused_computation.10.clone.1 | convolution fusion | flops 2419851264 | bytes 5251072 | tf_op jit(solution)/shard_map/while/body/eval_jaxpr/dot_general | solution.py:16
  161.9 4.8 %fusion.57 = f32[1536,512]{1,0:T(8,128)S(1)} fusion(f32[1536,256]{1,0:T(8,128)} %get-tuple-element.247, f32[512,256]{1,0:T(8,128)} %copy.9, f32[512]{0:T(512)S(1)} %multiply_reduce_fusion.8, f32[1536]{0:T(1024)S(1)} %get-tuple-element.246), kind=kOutput, calls=%fused_computation.10.clone.1 | convolution fusion | flops 2419851264 | bytes 5251072 | tf_op jit(solution)/shard_map/while/body/eval_jaxpr/dot_general | solution.py:16
  198.8 5.0 %fusion.17 = f32[1536,512]{1,0:T(8,128)S(1)} fusion(f32[512,256]{1,0:T(8,128)} %get-tuple-element.73, f32[1536,256]{1,0:T(8,128)} %get-tuple-element.276, f32[512]{0:T(512)S(1)} %multiply_reduce_fusion.4, f32[1536]{0:T(1024)S(1)} %get-tuple-element.282), kind=kOutput, calls=%fused_computation.25 | convolution fusion | flops 2419851264 | bytes 5251072 | tf_op jit(solution)/shard_map/dot_general | solution.py:16
  207.2 162.8 %while.29 = (s32[]{:T(128)}, f32[512,256]{1,0:T(8,128)S(1)}, f32[512]{0:T(512)S(1)}, f32[1536]{0:T(1024)S(1)}, f32[1536,256]{1,0:T(8,128)S(1)}, /*index=5*/f32[1536]{0:T(1024)}, f32[1536,1]{0,1:T(1,128)S(1)}, s32[]{:T(128)}) while((s32[]{:T(128)}, f32[512,256]{1,0:T(8,128)S(1)}, f32[512]{0:T(512)S(1)}, f32[1536]{0:T(1024)S(1)}, ...), condition=%wide.wide.region_7.0_spmd, body=%wide.wide.region_5.0_spmd.sunk | while | flops 2429550592 | bytes 12091557 | solution.py:60
  212.7 5.4 %collective-permute-done.3 = f32[512]{0:T(512)S(1)} collective-permute-done((f32[512]{0:T(512)S(1)}, f32[512]{0:T(512)S(1)}, u32[]{:S(2)}, u32[]{:S(2)}) %collective-permute-start.3) | collective-permute-done | bytes 2080 | tf_op jit(solution)/shard_map/while/body/eval_jaxpr/ppermute | solution.py:11
  223.5 5.4 %collective-permute-done.3 = f32[512]{0:T(512)S(1)} collective-permute-done((f32[512]{0:T(512)S(1)}, f32[512]{0:T(512)S(1)}, u32[]{:S(2)}, u32[]{:S(2)}) %collective-permute-start.3) | collective-permute-done | bytes 2080 | tf_op jit(solution)/shard_map/while/body/eval_jaxpr/ppermute | solution.py:11
  234.4 5.4 %collective-permute-done.3 = f32[512]{0:T(512)S(1)} collective-permute-done((f32[512]{0:T(512)S(1)}, f32[512]{0:T(512)S(1)}, u32[]{:S(2)}, u32[]{:S(2)}) %collective-permute-start.3) | collective-permute-done | bytes 2080 | tf_op jit(solution)/shard_map/while/body/eval_jaxpr/ppermute | solution.py:11
  245.2 5.4 %collective-permute-done.3 = f32[512]{0:T(512)S(1)} collective-permute-done((f32[512]{0:T(512)S(1)}, f32[512]{0:T(512)S(1)}, u32[]{:S(2)}, u32[]{:S(2)}) %collective-permute-start.3) | collective-permute-done | bytes 2080 | tf_op jit(solution)/shard_map/while/body/eval_jaxpr/ppermute | solution.py:11
  256.1 5.4 %collective-permute-done.3 = f32[512]{0:T(512)S(1)} collective-permute-done((f32[512]{0:T(512)S(1)}, f32[512]{0:T(512)S(1)}, u32[]{:S(2)}, u32[]{:S(2)}) %collective-permute-start.3) | collective-permute-done | bytes 2080 | tf_op jit(solution)/shard_map/while/body/eval_jaxpr/ppermute | solution.py:11
  266.9 5.4 %collective-permute-done.3 = f32[512]{0:T(512)S(1)} collective-permute-done((f32[512]{0:T(512)S(1)}, f32[512]{0:T(512)S(1)}, u32[]{:S(2)}, u32[]{:S(2)}) %collective-permute-start.3) | collective-permute-done | bytes 2080 | tf_op jit(solution)/shard_map/while/body/eval_jaxpr/ppermute | solution.py:11
  277.8 5.4 %collective-permute-done.3 = f32[512]{0:T(512)S(1)} collective-permute-done((f32[512]{0:T(512)S(1)}, f32[512]{0:T(512)S(1)}, u32[]{:S(2)}, u32[]{:S(2)}) %collective-permute-start.3) | collective-permute-done | bytes 2080 | tf_op jit(solution)/shard_map/while/body/eval_jaxpr/ppermute | solution.py:11
  288.6 5.4 %collective-permute-done.3 = f32[512]{0:T(512)S(1)} collective-permute-done((f32[512]{0:T(512)S(1)}, f32[512]{0:T(512)S(1)}, u32[]{:S(2)}, u32[]{:S(2)}) %collective-permute-start.3) | collective-permute-done | bytes 2080 | tf_op jit(solution)/shard_map/while/body/eval_jaxpr/ppermute | solution.py:11
  299.5 5.4 %collective-permute-done.3 = f32[512]{0:T(512)S(1)} collective-permute-done((f32[512]{0:T(512)S(1)}, f32[512]{0:T(512)S(1)}, u32[]{:S(2)}, u32[]{:S(2)}) %collective-permute-start.3) | collective-permute-done | bytes 2080 | tf_op jit(solution)/shard_map/while/body/eval_jaxpr/ppermute | solution.py:11
  310.3 5.4 %collective-permute-done.3 = f32[512]{0:T(512)S(1)} collective-permute-done((f32[512]{0:T(512)S(1)}, f32[512]{0:T(512)S(1)}, u32[]{:S(2)}, u32[]{:S(2)}) %collective-permute-start.3) | collective-permute-done | bytes 2080 | tf_op jit(solution)/shard_map/while/body/eval_jaxpr/ppermute | solution.py:11
  321.2 5.4 %collective-permute-done.3 = f32[512]{0:T(512)S(1)} collective-permute-done((f32[512]{0:T(512)S(1)}, f32[512]{0:T(512)S(1)}, u32[]{:S(2)}, u32[]{:S(2)}) %collective-permute-start.3) | collective-permute-done | bytes 2080 | tf_op jit(solution)/shard_map/while/body/eval_jaxpr/ppermute | solution.py:11
  332.0 5.4 %collective-permute-done.3 = f32[512]{0:T(512)S(1)} collective-permute-done((f32[512]{0:T(512)S(1)}, f32[512]{0:T(512)S(1)}, u32[]{:S(2)}, u32[]{:S(2)}) %collective-permute-start.3) | collective-permute-done | bytes 2080 | tf_op jit(solution)/shard_map/while/body/eval_jaxpr/ppermute | solution.py:11
  342.9 5.4 %collective-permute-done.3 = f32[512]{0:T(512)S(1)} collective-permute-done((f32[512]{0:T(512)S(1)}, f32[512]{0:T(512)S(1)}, u32[]{:S(2)}, u32[]{:S(2)}) %collective-permute-start.3) | collective-permute-done | bytes 2080 | tf_op jit(solution)/shard_map/while/body/eval_jaxpr/ppermute | solution.py:11
  353.7 5.4 %collective-permute-done.3 = f32[512]{0:T(512)S(1)} collective-permute-done((f32[512]{0:T(512)S(1)}, f32[512]{0:T(512)S(1)}, u32[]{:S(2)}, u32[]{:S(2)}) %collective-permute-start.3) | collective-permute-done | bytes 2080 | tf_op jit(solution)/shard_map/while/body/eval_jaxpr/ppermute | solution.py:11
  364.6 5.4 %collective-permute-done.3 = f32[512]{0:T(512)S(1)} collective-permute-done((f32[512]{0:T(512)S(1)}, f32[512]{0:T(512)S(1)}, u32[]{:S(2)}, u32[]{:S(2)}) %collective-permute-start.3) | collective-permute-done | bytes 2080 | tf_op jit(solution)/shard_map/while/body/eval_jaxpr/ppermute | solution.py:11
  375.0 5.1 %collective-permute-done.4 = f32[512]{0:T(512)S(1)} collective-permute-done((f32[512]{0:T(512)S(1)}, f32[512]{0:T(512)S(1)}, u32[]{:S(2)}, u32[]{:S(2)}) %collective-permute-start.4) | collective-permute-done | bytes 2080 | tf_op jit(solution)/shard_map/ppermute | solution.py:11
  380.1 25.3 %psum.7 = f32[512]{0:T(512)S(1)} all-reduce(f32[512]{0:T(512)S(1)} %collective-permute-done.4), channel_id=1, replica_groups=mesh['blk'=16,'rows'=8] {'rows'}, use_global_device_ids=true, to_apply=%region_9.0 | all-reduce | flops 512 | bytes 4096 | tf_op jit(solution)/shard_map/psum | solution.py:63
  (292 shorter events, 269.2 us)
Async XLA Ops:
  5.7 11.0 %collective-permute-start = (f32[512,256]{1,0:T(8,128)}, f32[512,256]{1,0:T(8,128)}, u32[]{:S(2)}, u32[]{:S(2)}) collective-permute-start(f32[512,256]{1,0:T(8,128)} %copy.9), channel_id=1, source_target_pairs={{0,8},{8,16},{16,24},{24,32},{32,40},{40,48},{48,56},{56,64},{64,7... | collective-permute-start | bytes 1572872 | tf_op jit(solution)/shard_map/while/body/eval_jaxpr/ppermute | solution.py:11
  5.7 11.0 %collective-permute-start.1 = (f32[512]{0:T(512)S(1)}, f32[512]{0:T(512)S(1)}, u32[]{:S(2)}, u32[]{:S(2)}) collective-permute-start(f32[512]{0:T(512)S(1)} %copy.10), channel_id=1, source_target_pairs={{0,8},{8,16},{16,24},{24,32},{32,40},{40,48},{48,56},{56,64},{64,7... | collective-permute-start | bytes 6152 | tf_op jit(solution)/shard_map/while/body/eval_jaxpr/ppermute | solution.py:11
  18.6 11.0 %collective-permute-start = (f32[512,256]{1,0:T(8,128)}, f32[512,256]{1,0:T(8,128)}, u32[]{:S(2)}, u32[]{:S(2)}) collective-permute-start(f32[512,256]{1,0:T(8,128)} %copy.9), channel_id=1, source_target_pairs={{0,8},{8,16},{16,24},{24,32},{32,40},{40,48},{48,56},{56,64},{64,7... | collective-permute-start | bytes 1572872 | tf_op jit(solution)/shard_map/while/body/eval_jaxpr/ppermute | solution.py:11
  18.6 11.0 %collective-permute-start.1 = (f32[512]{0:T(512)S(1)}, f32[512]{0:T(512)S(1)}, u32[]{:S(2)}, u32[]{:S(2)}) collective-permute-start(f32[512]{0:T(512)S(1)} %copy.10), channel_id=1, source_target_pairs={{0,8},{8,16},{16,24},{24,32},{32,40},{40,48},{48,56},{56,64},{64,7... | collective-permute-start | bytes 6152 | tf_op jit(solution)/shard_map/while/body/eval_jaxpr/ppermute | solution.py:11
  31.5 11.0 %collective-permute-start = (f32[512,256]{1,0:T(8,128)}, f32[512,256]{1,0:T(8,128)}, u32[]{:S(2)}, u32[]{:S(2)}) collective-permute-start(f32[512,256]{1,0:T(8,128)} %copy.9), channel_id=1, source_target_pairs={{0,8},{8,16},{16,24},{24,32},{32,40},{40,48},{48,56},{56,64},{64,7... | collective-permute-start | bytes 1572872 | tf_op jit(solution)/shard_map/while/body/eval_jaxpr/ppermute | solution.py:11
  31.5 11.0 %collective-permute-start.1 = (f32[512]{0:T(512)S(1)}, f32[512]{0:T(512)S(1)}, u32[]{:S(2)}, u32[]{:S(2)}) collective-permute-start(f32[512]{0:T(512)S(1)} %copy.10), channel_id=1, source_target_pairs={{0,8},{8,16},{16,24},{24,32},{32,40},{40,48},{48,56},{56,64},{64,7... | collective-permute-start | bytes 6152 | tf_op jit(solution)/shard_map/while/body/eval_jaxpr/ppermute | solution.py:11
  44.4 11.0 %collective-permute-start = (f32[512,256]{1,0:T(8,128)}, f32[512,256]{1,0:T(8,128)}, u32[]{:S(2)}, u32[]{:S(2)}) collective-permute-start(f32[512,256]{1,0:T(8,128)} %copy.9), channel_id=1, source_target_pairs={{0,8},{8,16},{16,24},{24,32},{32,40},{40,48},{48,56},{56,64},{64,7... | collective-permute-start | bytes 1572872 | tf_op jit(solution)/shard_map/while/body/eval_jaxpr/ppermute | solution.py:11
  57.3 11.0 %collective-permute-start = (f32[512,256]{1,0:T(8,128)}, f32[512,256]{1,0:T(8,128)}, u32[]{:S(2)}, u32[]{:S(2)}) collective-permute-start(f32[512,256]{1,0:T(8,128)} %copy.9), channel_id=1, source_target_pairs={{0,8},{8,16},{16,24},{24,32},{32,40},{40,48},{48,56},{56,64},{64,7... | collective-permute-start | bytes 1572872 | tf_op jit(solution)/shard_map/while/body/eval_jaxpr/ppermute | solution.py:11
  57.3 11.0 %collective-permute-start.1 = (f32[512]{0:T(512)S(1)}, f32[512]{0:T(512)S(1)}, u32[]{:S(2)}, u32[]{:S(2)}) collective-permute-start(f32[512]{0:T(512)S(1)} %copy.10), channel_id=1, source_target_pairs={{0,8},{8,16},{16,24},{24,32},{32,40},{40,48},{48,56},{56,64},{64,7... | collective-permute-start | bytes 6152 | tf_op jit(solution)/shard_map/while/body/eval_jaxpr/ppermute | solution.py:11
  70.3 11.0 %collective-permute-start = (f32[512,256]{1,0:T(8,128)}, f32[512,256]{1,0:T(8,128)}, u32[]{:S(2)}, u32[]{:S(2)}) collective-permute-start(f32[512,256]{1,0:T(8,128)} %copy.9), channel_id=1, source_target_pairs={{0,8},{8,16},{16,24},{24,32},{32,40},{40,48},{48,56},{56,64},{64,7... | collective-permute-start | bytes 1572872 | tf_op jit(solution)/shard_map/while/body/eval_jaxpr/ppermute | solution.py:11
  70.3 11.0 %collective-permute-start.1 = (f32[512]{0:T(512)S(1)}, f32[512]{0:T(512)S(1)}, u32[]{:S(2)}, u32[]{:S(2)}) collective-permute-start(f32[512]{0:T(512)S(1)} %copy.10), channel_id=1, source_target_pairs={{0,8},{8,16},{16,24},{24,32},{32,40},{40,48},{48,56},{56,64},{64,7... | collective-permute-start | bytes 6152 | tf_op jit(solution)/shard_map/while/body/eval_jaxpr/ppermute | solution.py:11
  83.2 11.0 %collective-permute-start = (f32[512,256]{1,0:T(8,128)}, f32[512,256]{1,0:T(8,128)}, u32[]{:S(2)}, u32[]{:S(2)}) collective-permute-start(f32[512,256]{1,0:T(8,128)} %copy.9), channel_id=1, source_target_pairs={{0,8},{8,16},{16,24},{24,32},{32,40},{40,48},{48,56},{56,64},{64,7... | collective-permute-start | bytes 1572872 | tf_op jit(solution)/shard_map/while/body/eval_jaxpr/ppermute | solution.py:11
  83.2 11.0 %collective-permute-start.1 = (f32[512]{0:T(512)S(1)}, f32[512]{0:T(512)S(1)}, u32[]{:S(2)}, u32[]{:S(2)}) collective-permute-start(f32[512]{0:T(512)S(1)} %copy.10), channel_id=1, source_target_pairs={{0,8},{8,16},{16,24},{24,32},{32,40},{40,48},{48,56},{56,64},{64,7... | collective-permute-start | bytes 6152 | tf_op jit(solution)/shard_map/while/body/eval_jaxpr/ppermute | solution.py:11
  96.1 11.0 %collective-permute-start = (f32[512,256]{1,0:T(8,128)}, f32[512,256]{1,0:T(8,128)}, u32[]{:S(2)}, u32[]{:S(2)}) collective-permute-start(f32[512,256]{1,0:T(8,128)} %copy.9), channel_id=1, source_target_pairs={{0,8},{8,16},{16,24},{24,32},{32,40},{40,48},{48,56},{56,64},{64,7... | collective-permute-start | bytes 1572872 | tf_op jit(solution)/shard_map/while/body/eval_jaxpr/ppermute | solution.py:11
  96.1 11.0 %collective-permute-start.1 = (f32[512]{0:T(512)S(1)}, f32[512]{0:T(512)S(1)}, u32[]{:S(2)}, u32[]{:S(2)}) collective-permute-start(f32[512]{0:T(512)S(1)} %copy.10), channel_id=1, source_target_pairs={{0,8},{8,16},{16,24},{24,32},{32,40},{40,48},{48,56},{56,64},{64,7... | collective-permute-start | bytes 6152 | tf_op jit(solution)/shard_map/while/body/eval_jaxpr/ppermute | solution.py:11
  109.0 11.0 %collective-permute-start = (f32[512,256]{1,0:T(8,128)}, f32[512,256]{1,0:T(8,128)}, u32[]{:S(2)}, u32[]{:S(2)}) collective-permute-start(f32[512,256]{1,0:T(8,128)} %copy.9), channel_id=1, source_target_pairs={{0,8},{8,16},{16,24},{24,32},{32,40},{40,48},{48,56},{56,64},{64,7... | collective-permute-start | bytes 1572872 | tf_op jit(solution)/shard_map/while/body/eval_jaxpr/ppermute | solution.py:11
  109.0 11.0 %collective-permute-start.1 = (f32[512]{0:T(512)S(1)}, f32[512]{0:T(512)S(1)}, u32[]{:S(2)}, u32[]{:S(2)}) collective-permute-start(f32[512]{0:T(512)S(1)} %copy.10), channel_id=1, source_target_pairs={{0,8},{8,16},{16,24},{24,32},{32,40},{40,48},{48,56},{56,64},{64,7... | collective-permute-start | bytes 6152 | tf_op jit(solution)/shard_map/while/body/eval_jaxpr/ppermute | solution.py:11
  122.0 11.0 %collective-permute-start = (f32[512,256]{1,0:T(8,128)}, f32[512,256]{1,0:T(8,128)}, u32[]{:S(2)}, u32[]{:S(2)}) collective-permute-start(f32[512,256]{1,0:T(8,128)} %copy.9), channel_id=1, source_target_pairs={{0,8},{8,16},{16,24},{24,32},{32,40},{40,48},{48,56},{56,64},{64,7... | collective-permute-start | bytes 1572872 | tf_op jit(solution)/shard_map/while/body/eval_jaxpr/ppermute | solution.py:11
  122.0 11.0 %collective-permute-start.1 = (f32[512]{0:T(512)S(1)}, f32[512]{0:T(512)S(1)}, u32[]{:S(2)}, u32[]{:S(2)}) collective-permute-start(f32[512]{0:T(512)S(1)} %copy.10), channel_id=1, source_target_pairs={{0,8},{8,16},{16,24},{24,32},{32,40},{40,48},{48,56},{56,64},{64,7... | collective-permute-start | bytes 6152 | tf_op jit(solution)/shard_map/while/body/eval_jaxpr/ppermute | solution.py:11
  134.9 11.0 %collective-permute-start = (f32[512,256]{1,0:T(8,128)}, f32[512,256]{1,0:T(8,128)}, u32[]{:S(2)}, u32[]{:S(2)}) collective-permute-start(f32[512,256]{1,0:T(8,128)} %copy.9), channel_id=1, source_target_pairs={{0,8},{8,16},{16,24},{24,32},{32,40},{40,48},{48,56},{56,64},{64,7... | collective-permute-start | bytes 1572872 | tf_op jit(solution)/shard_map/while/body/eval_jaxpr/ppermute | solution.py:11
  147.8 11.0 %collective-permute-start = (f32[512,256]{1,0:T(8,128)}, f32[512,256]{1,0:T(8,128)}, u32[]{:S(2)}, u32[]{:S(2)}) collective-permute-start(f32[512,256]{1,0:T(8,128)} %copy.9), channel_id=1, source_target_pairs={{0,8},{8,16},{16,24},{24,32},{32,40},{40,48},{48,56},{56,64},{64,7... | collective-permute-start | bytes 1572872 | tf_op jit(solution)/shard_map/while/body/eval_jaxpr/ppermute | solution.py:11
  160.7 11.0 %collective-permute-start = (f32[512,256]{1,0:T(8,128)}, f32[512,256]{1,0:T(8,128)}, u32[]{:S(2)}, u32[]{:S(2)}) collective-permute-start(f32[512,256]{1,0:T(8,128)} %copy.9), channel_id=1, source_target_pairs={{0,8},{8,16},{16,24},{24,32},{32,40},{40,48},{48,56},{56,64},{64,7... | collective-permute-start | bytes 1572872 | tf_op jit(solution)/shard_map/while/body/eval_jaxpr/ppermute | solution.py:11
  173.6 11.0 %collective-permute-start = (f32[512,256]{1,0:T(8,128)}, f32[512,256]{1,0:T(8,128)}, u32[]{:S(2)}, u32[]{:S(2)}) collective-permute-start(f32[512,256]{1,0:T(8,128)} %copy.9), channel_id=1, source_target_pairs={{0,8},{8,16},{16,24},{24,32},{32,40},{40,48},{48,56},{56,64},{64,7... | collective-permute-start | bytes 1572872 | tf_op jit(solution)/shard_map/while/body/eval_jaxpr/ppermute | solution.py:11
  186.6 11.0 %collective-permute-start = (f32[512,256]{1,0:T(8,128)}, f32[512,256]{1,0:T(8,128)}, u32[]{:S(2)}, u32[]{:S(2)}) collective-permute-start(f32[512,256]{1,0:T(8,128)} %copy.9), channel_id=1, source_target_pairs={{0,8},{8,16},{16,24},{24,32},{32,40},{40,48},{48,56},{56,64},{64,7... | collective-permute-start | bytes 1572872 | tf_op jit(solution)/shard_map/while/body/eval_jaxpr/ppermute | solution.py:11
  (42 other events, 339.0 us)
where the time goes:
time: 408 us; the launch traced here: 406 us
  matrix products  202 us (50%)
  waiting for transfers between devices  116 us (28%)
  local copies, waits for them, and re-layouts  31.3 us (8%)
  blocking collectives  25.3 us (6%)
  other arithmetic  24 us (6%)
  starting transfers between devices  5.51 us (1%)
    dot_general x32, matrix products, kernel_block(): jnp.dot(points, block.T, precision=lax.Precision.HIGHEST, preferred_eleme...  130 us
    ppermute x61, waiting for transfers between devices, passed_along(): return lax.ppermute(x, axis, [(i, (i + by) % peers) for i in range(peers)])  116 us
    dot_general x16, matrix products, apply_block(): jnp.dot(kernel, coef, precision=lax.Precision.HIGHEST, preferred_element_...  44.4 us
    while x30, local copies, waits for them, and re-layouts  28.3 us
    dot_general x16, matrix products, transpose_block(): jnp.dot(point_values, kernel, precision=lax.Precision.HIGHEST, preferred_...  27.7 us
    psum x1, blocking collectives, body(): summed = lax.psum(owned, 'rows')  25.3 us
    reduce_sum x32, other arithmetic, kernel_block(): block_sq = jnp.sum(block * block, axis=1)  21.4 us
  transfers between devices with their start and end apart: 61, of which 31 were waited for; matrix products, arithmetic and copies ran while one was open for 52% of the time, Pallas kernels for 0%

commit v1 on v0

v1 whole, which is shorter than its diff:
```python
import functools
import math

import jax
import jax.numpy as jnp
from jax import lax
from jax.experimental import pallas as pl
from jax.experimental.pallas import tpu as pltpu
from jax.sharding import PartitionSpec as P

F32, BF16, F8 = jnp.float32, jnp.bfloat16, jnp.float8_e4m3fn
LOG2E = 1.4426950408889634
UNIT = 256
PACKED = 264
LIFT = 256.0
ROWS = 256
VMEM = pl.BlockSpec(memory_space=pltpu.VMEM)
HBM = pl.BlockSpec(memory_space=pltpu.HBM)


def constants(width):
    scale = LOG2E / math.sqrt(width)
    return scale, 0.5 * LOG2E * math.sqrt(width)


def prepare_points(x_ref, xh_ref, x8_ref, a_ref):
    scale, offset = constants(x_ref.shape[1])
    for q in range(0, x_ref.shape[0], ROWS):
        r = slice(q, q + ROWS)
        x = x_ref[r, :]
        high = x.astype(BF16)
        low = (x - high.astype(F32)) * LIFT
        xh_ref[r, :] = high
        x8_ref[r, :] = jnp.concatenate([x.astype(F8), low.astype(F8)], axis=1)
        a = jnp.sum(x * x, axis=1, keepdims=True) * (-0.5 * scale) + offset
        a_ref[r, :] = jnp.broadcast_to(a, (ROWS, 128))


def prepare_units(refs, wh_ref, w8_ref, b_ref, c_ref):
    i = 0
    for ref in refs:
        for j in range(ref.shape[0]):
            width = ref.shape[2]
            scale, offset = constants(width)
            t = ref[j, 0:UNIT, :].T
            scaled = t * scale
            high = scaled.astype(BF16)
            low = (scaled - high.astype(F32)) * (LIFT / scale)
            wh_ref[i] = high
            w8_ref[i] = jnp.concatenate([low.astype(F8), t.astype(F8)], axis=0)
            b_ref[i] = jnp.sum(t * t, axis=0, keepdims=True) * (-0.5 * scale) + offset
            c_ref[i] = ref[j, UNIT : UNIT + 1, :]
            i += 1


def tile(i, r, xh_ref, x8_ref, a_ref, wh_ref, w8_ref, b_ref, c_ref, k_ref):
    scale, _ = constants(xh_ref.shape[1])
    main = jnp.dot(xh_ref[r, :], wh_ref[i], preferred_element_type=F32)
    cross = jnp.dot(x8_ref[r, :], w8_ref[i], preferred_element_type=F32)
    a = a_ref[r, :]
    value = None
    for t in range(0, UNIT, 128):
        c = slice(t, t + 128)
        k = jnp.exp2(main[:, c] + cross[:, c] * (scale / LIFT) + a + b_ref[i, :, c])
        k_ref[i, r, c] = k
        term = k * c_ref[i, :, c]
        value = term if value is None else value + term
    return value


def first_product(group, points, prepared, v_in, v_ref, k_ref, saved=None, sem=None):
    units = k_ref.shape[0]
    assert units % group == 0
    rows = points[0].shape[0]

    def save(j, q):
        part = (pl.ds(j * group, group), pl.ds(q, ROWS))
        return pltpu.make_async_copy(k_ref.at[part], saved.at[part], sem)

    @pl.loop(0, units // group)
    def _(j):
        for q in range(0, rows, ROWS):
            r = slice(q, q + ROWS)
            value = None
            for u in range(group):
                term = tile(j * group + u, r, *points, *prepared, k_ref)
                value = term if value is None else value + term
            if v_in is None:
                before = jnp.where(j == 0, 0.0, v_ref[r, :])
            else:
                before = jnp.where(j == 0, v_in[r, :], v_ref[r, :])
            v_ref[r, :] = before + value
            if saved is not None:
                save(j, q).start()

    if saved is not None:
        pltpu.make_async_copy(k_ref, saved, sem).wait()


def opening_kernel(x_ref, *rest):
    units, (xh, x8, a, v, saved), (k, *prepared), sem = rest[:2], rest[2:7], rest[7:12], rest[12]
    prepare_points(x_ref, xh, x8, a)
    prepare_units(units, *prepared)
    v[...] = jnp.zeros_like(v)
    first_product(2, (xh, x8, a), prepared, None, v, k, saved, sem)


def middle_kernel(n, group, xh, x8, a, v_in, *rest):
    units, (v, saved), (k, *prepared), sem = rest[:n], rest[n : n + 2], rest[n + 2 : n + 7], rest[n + 7]
    prepare_units(units, *prepared)
    v[...] = v_in[...]
    first_product(group, (xh, x8, a), prepared, v_in, v, k, saved, sem)


def closing_kernel(n, m, group, place_ref, xh, x8, a, v_in, *rest):
    units, saved, out = rest[:n], rest[n : n + m], rest[n + m]
    v, sums, k, *more = rest[n + m + 1 :]
    prepared, held, sem = more[:4], more[4 : 4 + m], more[4 + m]
    copies = [pltpu.make_async_copy(saved[i], held[i], sem.at[i]) for i in range(m)]
    for copy in copies:
        copy.start()
    prepare_units(units, *prepared)
    first_product(group, (xh, x8, a), prepared, v_in, v, k)
    for q in range(0, v.shape[0], ROWS):
        r = slice(q, q + ROWS)
        v[r, :] = jnp.broadcast_to(jnp.sum(v[r, :], axis=1, keepdims=True), (ROWS, 128))
    second_product(k, v, sums, 0)
    at = k.shape[0]
    for copy, part in zip(copies, held):
        copy.wait()
        second_product(part, v, sums, at)
        at += part.shape[0]
    copies_out = out.shape[1]
    for i in range(place_ref.shape[0]):
        for h in range(2):
            row = sums[2 * i + h]
            for j in range(copies_out):
                out[place_ref[i], j, :, h * UNIT : (h + 1) * UNIT] = row


def second_product(k_ref, v_ref, sums, at):
    group = 2
    rows = v_ref.shape[0]
    lanes = [slice(t, t + 128) for t in range(0, UNIT, 128)]

    @pl.loop(0, k_ref.shape[0] // group)
    def _(j):
        total = [[jnp.zeros((8, 128), F32) for _ in lanes] for _ in range(group)]
        for q in range(0, rows, 8):
            v = v_ref[q : q + 8, :]
            for u in range(group):
                for t, c in enumerate(lanes):
                    total[u][t] = total[u][t] + k_ref[j * group + u, q : q + 8, c] * v
        for u in range(group):
            for t, c in enumerate(lanes):
                sums[at + j * group + u, :, c] = jnp.sum(total[u][t], axis=0, keepdims=True)


def prepared_scratch(n, width):
    return [
        pltpu.VMEM((n, width, UNIT), BF16),
        pltpu.VMEM((n, 2 * width, UNIT), F8),
        pltpu.VMEM((n, 1, UNIT), F32),
        pltpu.VMEM((n, 1, UNIT), F32),
    ]


def cost(rows, n, width):
    return pl.CostEstimate(
        flops=8 * rows * n * UNIT * width, bytes_accessed=rows * n * UNIT * 4, transcendentals=rows * n * UNIT
    )


def of(shape, dtype=F32):
    return jax.ShapeDtypeStruct(shape, dtype)


def count(blocks):
    return sum(b.shape[0] for b in blocks)


def opening(x, blocks):
    rows, width = x.shape
    n = count(blocks)
    return pl.pallas_call(
        opening_kernel,
        in_specs=[VMEM] * 3,
        out_specs=[VMEM] * 4 + [HBM],
        out_shape=[of((rows, width), BF16), of((rows, 2 * width), F8), of((rows, 128)), of((rows, 128)), of((n, rows, UNIT))],
        scratch_shapes=[pltpu.VMEM((n, rows, UNIT), F32), *prepared_scratch(n, width), pltpu.SemaphoreType.DMA],
        cost_estimate=cost(rows, n, width),
        compiler_params=pltpu.CompilerParams(vmem_limit_bytes=58 << 20),
        name="opening",
    )(x, *blocks)


def middle(group, xh, x8, a, v, blocks):
    rows, width = xh.shape
    n = count(blocks)
    return pl.pallas_call(
        functools.partial(middle_kernel, len(blocks), group),
        in_specs=[VMEM] * (4 + len(blocks)),
        out_specs=[VMEM, HBM],
        out_shape=[of((rows, 128)), of((n, rows, UNIT))],
        scratch_shapes=[pltpu.VMEM((n, rows, UNIT), F32), *prepared_scratch(n, width), pltpu.SemaphoreType.DMA],
        cost_estimate=cost(rows, n, width),
        compiler_params=pltpu.CompilerParams(vmem_limit_bytes=40 << 20),
        name="middle",
    )(xh, x8, a, v, *blocks)


def closing(group, place, copies, xh, x8, a, v, blocks, saved):
    rows, width = xh.shape
    n = count(blocks)
    total = n + count(saved)
    return pl.pallas_call(
        functools.partial(closing_kernel, len(blocks), len(saved), group),
        in_specs=[pl.BlockSpec(memory_space=pltpu.SMEM)] + [VMEM] * (4 + len(blocks)) + [HBM] * len(saved),
        out_specs=VMEM,
        out_shape=of((total // 2, copies, 1, 2 * UNIT)),
        scratch_shapes=[
            pltpu.VMEM((rows, 128), F32),
            pltpu.VMEM((total, 1, UNIT), F32),
            pltpu.VMEM((n, rows, UNIT), F32),
            *prepared_scratch(n, width),
            *[pltpu.VMEM(k.shape, F32) for k in saved],
            pltpu.SemaphoreType.DMA((len(saved),)),
        ],
        cost_estimate=cost(rows, 2 * n, width),
        compiler_params=pltpu.CompilerParams(vmem_limit_bytes=60 << 20),
        name="closing",
    )(place, xh, x8, a, v, *blocks, *saved)


RING, PAIR, CORES = 4, 2, 2


def index(x, z, core):
    return ((x % RING) * PAIR + z % PAIR) * CORES + core % CORES


def fetch(array, x=0, z=0, core=0):
    pairs = [
        (index(i + x, j + z, k + core), index(i, j, k))
        for i in range(RING)
        for j in range(PAIR)
        for k in range(CORES)
    ]
    return lax.ppermute(array, "blk", pairs)


def body(points, centres, coefficients):
    rows_size = lax.axis_size("rows")
    width = centres.shape[1]
    total_points = points.shape[0] * lax.axis_size("blk") * rows_size
    units = centres.shape[0] // UNIT
    own = jnp.concatenate(
        [
            centres.reshape(units, UNIT, width),
            coefficients.reshape(units, 1, UNIT),
            jnp.zeros((units, PACKED - UNIT - 1, width), F32),
        ],
        axis=1,
    )
    me = lax.axis_index("blk")
    at_x, at_z, at_core = me // (PAIR * CORES), me // CORES % PAIR, me % CORES

    def place(x, z, core):
        return index(at_x + x, at_z + z, at_core + core)

    def other(array):
        return fetch(array, core=1)

    after = lax.optimization_barrier
    near = [fetch(own, x=1), fetch(own, x=-1), fetch(own, z=1)]
    beside = other(own)
    xh, x8, a, v, k0 = opening(points, [own, beside])
    *near, v = after((*near, v))
    up, down, across = near
    near_other = [other(b) for b in near]
    far = [fetch(up, x=1), fetch(across, x=-1), fetch(up, z=1)]
    v, k1 = middle(4, xh, x8, a, v, near + near_other)
    *far, v = after((*far, v))
    far_other = [other(b) for b in far]
    last = [fetch(far[2][0:1], x=1), fetch(far[1][1:2], x=-1)]
    v, k2 = middle(3, xh, x8, a, v, far)
    *last, v = after((*last, v))
    last_other = [other(b) for b in last]
    order = [(2, 0, 1), (-1, 1, 1), (1, 1, 1), (2, 1, 0), (2, 1, 1)]
    order += [(0, 0, 0), (0, 0, 1)]
    order += [(1, 0, 0), (-1, 0, 0), (0, 1, 0), (1, 0, 1), (-1, 0, 1), (0, 1, 1)]
    order += [(2, 0, 0), (-1, 1, 0), (1, 1, 0)]
    places = jnp.stack([place(*o) for o in order]).astype(jnp.int32)
    sums = closing(5, places, rows_size, xh, x8, a, v, far_other + last + last_other, [k0, k1, k2])
    parts = lax.all_to_all(sums.reshape(-1, 1, 2 * UNIT), ("blk", "rows"), 0, 0, tiled=True)
    return jnp.sum(parts, axis=(0, 1)) / total_points


def solution(mesh):
    return jax.shard_map(
        body,
        mesh=mesh,
        in_specs=(P(("blk", "rows"), None), P("blk", None), P("blk")),
        out_specs=P("blk"),
        check_vma=False,
    )
```

time: 408 us -> 89 us (0.22)
  matrix products: 202 us -> 0 us
  waiting for transfers between devices: 116 us -> 11.6 us
  Pallas kernels: 0 us -> 35.6 us
  local copies, waits for them, and re-layouts: 31.3 us -> 6.96 us
  other arithmetic: 24 us -> 1.95 us
  starting transfers between devices: 5.51 us -> 12.6 us
  blocking collectives: 25.3 us -> 18.8 us
    dot_general x64 -> x0, matrix products: 202 us -> none  [the longest x32 130 us: kernel_block(): jnp.dot(points, block.T, precision=lax.Precision.HIGHEST, preferred_eleme...]
    ppermute x61 -> x17, waiting for transfers between devices: 116 us -> 11.6 us  [fetch(): return lax.ppermute(array, 'blk', pairs)]
    pallas_call x0 -> x4, Pallas kernels: none -> 35.6 us  [the longest x1 15.6 us: closing(): pl.pallas_call(functools.partial(closing_kernel, len(blocks), len(saved),...]
    while x30 -> x0, local copies, waits for them, and re-layouts: 28.3 us -> none
    psum x1 -> x0, blocking collectives: 25.3 us -> none  [body(): summed = lax.psum(owned, 'rows')]
    reduce_sum x33 -> x1, other arithmetic: 23.2 us -> 0.21 us  [body(): return jnp.sum(parts, axis=(0, 1)) / total_points]
    all_to_all x0 -> x1, blocking collectives: none -> 18.8 us  [body(): lax.all_to_all(sums.reshape(-1, 1, 2 * UNIT), ('blk', 'rows'), 0, 0, tile...]
    ppermute x61 -> x17, starting transfers between devices: 5.51 us -> 12.6 us  [fetch(): return lax.ppermute(array, 'blk', pairs)]
  transfers between devices with their start and end apart: 61 -> 17, of which waited for: 31 -> 7; matrix products, arithmetic and copies ran while one was open for 52% -> 1% of each run, Pallas kernels for 0% -> 23%
where the time goes in v1:
time: 89 us; the launch traced here: 87.6 us
  Pallas kernels  35.6 us (40%)
  blocking collectives  18.8 us (21%)
  starting transfers between devices  12.6 us (14%)
  waiting for transfers between devices  11.6 us (13%)
  local copies, waits for them, and re-layouts  6.96 us (8%)
  other arithmetic  1.95 us (2%)
    all_to_all x1, blocking collectives, body(): lax.all_to_all(sums.reshape(-1, 1, 2 * UNIT), ('blk', 'rows'), 0, 0, tile...  18.8 us
    pallas_call x1, Pallas kernels, closing(): pl.pallas_call(functools.partial(closing_kernel, len(blocks), len(saved),...  15.6 us
    pallas_call x2, Pallas kernels, middle(): pl.pallas_call(functools.partial(middle_kernel, len(blocks), group), in_s...  12.8 us
    ppermute x17, starting transfers between devices, fetch(): return lax.ppermute(array, 'blk', pairs)  12.6 us
    ppermute x17, waiting for transfers between devices, fetch(): return lax.ppermute(array, 'blk', pairs)  11.6 us
    pallas_call x1, Pallas kernels, opening(): pl.pallas_call(opening_kernel, in_specs=[VMEM] * 3, out_specs=[VMEM] * 4...  7.23 us
    unnamed x22, local copies, waits for them, and re-layouts  6.24 us
  transfers between devices with their start and end apart: 17, of which 7 were waited for; matrix products, arithmetic and copies ran while one was open for 1% of the time, Pallas kernels for 23%

profile of v1, /device:TPU:0, one launch (start us, length us, event | category | flops | bytes accessed | tf_op | source)
XLA Modules:
  0.0 87.6 jit_solution(15877257213666702169)
XLA Ops:
  0.1 1.2 %maximum_maximum_fusion.rest_0_ = f32[2,264,256]{2,1,0:T(8,128)S(1)} fusion(f32[2,1,256]{2,1,0:T(1,128)} %bitcast.21, f32[2,256,256]{2,1,0:T(8,128)} %bitcast.19, f32[264]{0:T(512)S(1)} %pad.2.clone), kind=kLoop, calls=%fused_computation | loop fusion | flops 270336 | bytes 1068064 | tf_op jit(solution)/shard_map/concatenate | solution.py:257
  1.3 2.9 %collective-permute-start.1 = (f32[2,264,256]{2,1,0:T(8,128)S(1)}, f32[2,264,256]{2,1,0:T(8,128)S(1)}, u32[]{:S(2)}, u32[]{:S(2)}) collective-permute-start(f32[2,264,256]{2,1,0:T(8,128)S(1)} %maximum_maximum_fusion.rest_0_), channel_id=1, source_target_pairs={{32,0},{40,8},{48,16},{56,24},{64,32},{72,40},{80,48},{88,56},{96,... | collective-permute-start | bytes 1622024 | tf_op jit(solution)/shard_map/ppermute | solution.py:249
  4.3 1.9 %collective-permute-start.3 = (f32[2,264,256]{2,1,0:T(8,128)S(1)}, f32[2,264,256]{2,1,0:T(8,128)S(1)}, u32[]{:S(2)}, u32[]{:S(2)}) collective-permute-start(f32[2,264,256]{2,1,0:T(8,128)S(1)} %maximum_maximum_fusion.rest_0_), channel_id=1, source_target_pairs={{16,0},{24,8},{0,16},{8,24},{48,32},{56,40},{32,48},{40,56},{80,64... | collective-permute-start | bytes 1622024 | tf_op jit(solution)/shard_map/ppermute | solution.py:249
  6.2 0.8 copy-done.9
  7.0 7.2 %opening.1 = (bf16[1536,256]{1,0:T(8,128)(2,1)}, f8e4m3fn[1536,512]{1,0:T(32,128)(4,1)}, f32[1536,128]{1,0:T(8,128)}, f32[1536,128]{1,0:T(8,128)}, f32[4,1536,256]{2,1,0:T(8,128)}) custom-call(f32[1536,256]{1,0:T(8,128)} %x_ref.1, f32[2,264,256]{2,1,0:T(8,128)} %copy-done.5, f32[2,264,256]{2,1,0:T(8,128)} %copy-done.9), custom_call_target="tpu_custom_call" | custom-call | flops 3221225472 | bytes 6291456 | tf_op jit(solution)/shard_map/opening/pallas_call | solution.py:185
  14.2 2.2 %collective-permute-done.1.rest_0_ = f32[2,264,256]{2,1,0:T(8,128)S(1)} collective-permute-done((f32[2,264,256]{2,1,0:T(8,128)S(1)}, f32[2,264,256]{2,1,0:T(8,128)S(1)}, u32[]{:S(2)}, u32[]{:S(2)}) %collective-permute-start.1) | collective-permute-done | bytes 540704 | tf_op jit(solution)/shard_map/ppermute | solution.py:249
  16.4 3.4 %collective-permute-done.2.rest_1_ = f32[2,264,256]{2,1,0:T(8,128)S(1)} collective-permute-done((f32[2,264,256]{2,1,0:T(8,128)S(1)}, f32[2,264,256]{2,1,0:T(8,128)S(1)}, u32[]{:S(2)}, u32[]{:S(2)}) %collective-permute-start.2) | collective-permute-done | bytes 540704 | tf_op jit(solution)/shard_map/ppermute | solution.py:249
  20.3 1.9 %collective-permute-start.4 = (f32[2,264,256]{2,1,0:T(8,128)S(1)}, f32[2,264,256]{2,1,0:T(8,128)S(1)}, u32[]{:S(2)}, u32[]{:S(2)}) collective-permute-start(f32[2,264,256]{2,1,0:T(8,128)S(1)} %collective-permute-done.1.rest_0_), channel_id=1, source_target_pairs={{32,0},{40,8},{48,16},{56,24},{64,32},{72,40},{80,48},{88,56},{96,... | collective-permute-start | bytes 1622024 | tf_op jit(solution)/shard_map/ppermute | solution.py:249
  22.4 1.9 %collective-permute-start.6 = (f32[2,264,256]{2,1,0:T(8,128)S(1)}, f32[2,264,256]{2,1,0:T(8,128)S(1)}, u32[]{:S(2)}, u32[]{:S(2)}) collective-permute-start(f32[2,264,256]{2,1,0:T(8,128)S(1)} %collective-permute-done.1.rest_0_), channel_id=1, source_target_pairs={{16,0},{24,8},{0,16},{8,24},{48,32},{56,40},{32,48},{40,56},{80,64... | collective-permute-start | bytes 1622024 | tf_op jit(solution)/shard_map/ppermute | solution.py:249
  24.3 1.1 %copy-done = bf16[1536,256]{1,0:T(8,128)(2,1)S(1)} copy-done((bf16[1536,256]{1,0:T(8,128)(2,1)S(1)}, bf16[1536,256]{1,0:T(8,128)(2,1)}, u32[]{:S(2)}) %copy-start) | copy-done | bytes 786456
  25.4 1.1 %copy-done.1 = f8e4m3fn[1536,512]{1,0:T(32,128)(4,1)S(1)} copy-done((f8e4m3fn[1536,512]{1,0:T(32,128)(4,1)S(1)}, f8e4m3fn[1536,512]{1,0:T(32,128)(4,1)}, u32[]{:S(2)}) %copy-start.1) | copy-done | bytes 786456
  26.6 1.1 %copy-done.2 = f32[1536,128]{1,0:T(8,128)S(1)} copy-done((f32[1536,128]{1,0:T(8,128)S(1)}, f32[1536,128]{1,0:T(8,128)}, u32[]{:S(2)}) %copy-start.2) | copy-done | bytes 786456
  27.7 1.1 %copy-done.3 = f32[1536,128]{1,0:T(8,128)S(1)} copy-done((f32[1536,128]{1,0:T(8,128)S(1)}, f32[1536,128]{1,0:T(8,128)}, u32[]{:S(2)}) %copy-start.3) | copy-done | bytes 786456
  28.8 8.1 %middle.2 = (f32[1536,128]{1,0:T(8,128)S(1)}, f32[12,1536,256]{2,1,0:T(8,128)}) custom-call(bf16[1536,256]{1,0:T(8,128)(2,1)S(1)} %copy-done, f8e4m3fn[1536,512]{1,0:T(32,128)(4,1)S(1)} %copy-done.1, f32[1536,128]{1,0:T(8,128)S(1)} %copy-done.2, f32[1536,128]{1,0:T(8,128)S(1)} %copy-done.3, f32[2,264,256]{2,1,0:T(8,128)S(1)} %collective-permute-done.1.rest_0_, ...), custom_call_target="tpu_custom_call" | custom-call | flops 9663676416 | bytes 18874368 | tf_op jit(solution)/shard_map/middle/pallas_call | solution.py:200
  36.9 1.0 %collective-permute-done.5.rest_1_ = f32[2,264,256]{2,1,0:T(8,128)S(1)} collective-permute-done((f32[2,264,256]{2,1,0:T(8,128)S(1)}, f32[2,264,256]{2,1,0:T(8,128)S(1)}, u32[]{:S(2)}, u32[]{:S(2)}) %collective-permute-start.5) | collective-permute-done | bytes 540704 | tf_op jit(solution)/shard_map/ppermute | solution.py:249
  38.6 2.0 %collective-permute-start.10 = (f32[1,264,256]{2,1,0:T(8,128)S(1)}, f32[1,264,256]{2,1,0:T(8,128)S(1)}, u32[]{:S(2)}, u32[]{:S(2)}) collective-permute-start(f32[1,264,256]{2,1,0:T(8,128)S(1)} %slice.6), channel_id=1, source_target_pairs={{32,0},{40,8},{48,16},{56,24},{64,32},{72,40},{80,48},{88,56},{96,... | collective-permute-start | bytes 811016 | tf_op jit(solution)/shard_map/ppermute | solution.py:249
  40.6 4.7 %middle.3 = (f32[1536,128]{1,0:T(8,128)S(1)}, f32[6,1536,256]{2,1,0:T(8,128)}) custom-call(bf16[1536,256]{1,0:T(8,128)(2,1)S(1)} %copy-done, f8e4m3fn[1536,512]{1,0:T(32,128)(4,1)S(1)} %copy-done.1, f32[1536,128]{1,0:T(8,128)S(1)} %copy-done.2, f32[1536,128]{1,0:T(8,128)S(1)} %get-tuple-element.36.v_in, f32[2,264,256]{2,1,0:T(8,128)S(1)} %collective-permute-done.4.rest_0_, ...), custom_call_target="tpu_custom_call" | custom-call | flops 4831838208 | bytes 9437184 | tf_op jit(solution)/shard_map/middle/pallas_call | solution.py:200
  45.3 0.9 %copy-done.4 = f32[1536,128]{1,0:T(8,128)} copy-done((f32[1536,128]{1,0:T(8,128)}, f32[1536,128]{1,0:T(8,128)S(1)}, u32[]{:S(2)}) %copy-start.4) | copy-done | bytes 786456
  46.2 0.8 collective-permute-done.10.rest_3_
  47.1 3.1 %collective-permute-done.11.rest_4_ = f32[1,264,256]{2,1,0:T(8,128)} collective-permute-done((f32[1,264,256]{2,1,0:T(8,128)S(1)}, f32[1,264,256]{2,1,0:T(8,128)}, u32[]{:S(2)}, u32[]{:S(2)}) %collective-permute-start.11) | collective-permute-done | bytes 270368 | tf_op jit(solution)/shard_map/ppermute | solution.py:249
  50.6 0.6 stack.67.place_ref
  51.3 0.9 collective-permute-done.15.rest_5_
  52.4 15.6 %closing.1 = f32[16,8,1,512]{3,2,1,0:T(1,128)} custom-call(s32[16]{0:T(128)} %stack.67.place_ref, bf16[1536,256]{1,0:T(8,128)(2,1)} %get-tuple-element.25.xh, f8e4m3fn[1536,512]{1,0:T(32,128)(4,1)} %get-tuple-element.26.x8, f32[1536,128]{1,0:T(8,128)} %get-tuple-element.27.a, f32[1536,128]{1,0:T(8,128)} %copy-done.4, f32[2,264,256]{2,1,0:T(8,128)} %copy-done.8, ...), custom_call_target="tpu_custom_call" | custom-call | flops 16106127360 | bytes 31457280 | tf_op jit(solution)/shard_map/closing/pallas_call | solution.py:216
  68.0 18.8 %all_to_all.5 = f32[128,1,512]{2,1,0:T(1,128)S(1)} all-to-all(f32[128,1,512]{2,1,0:T(1,128)} %bitcast.20), channel_id=1, replica_groups=mesh['blk'=16,'rows'=8] {'blk','rows'}, dimensions={0} | all-to-all | bytes 524288 | tf_op jit(solution)/shard_map/all_to_all | solution.py:295
  (45 shorter events, 3.1 us)
Async XLA Ops:
  1.2 4.9 %copy-start.5 = (f32[2,264,256]{2,1,0:T(8,128)}, f32[2,264,256]{2,1,0:T(8,128)S(1)}, u32[]{:S(2)}) copy-start(f32[2,264,256]{2,1,0:T(8,128)S(1)} %maximum_maximum_fusion.rest_0_) | copy-start | bytes 1622020
  1.3 4.9 %collective-permute-start = (f32[2,264,256]{2,1,0:T(8,128)S(1)}, f32[2,264,256]{2,1,0:T(8,128)S(1)}, u32[]{:S(2)}, u32[]{:S(2)}) collective-permute-start(f32[2,264,256]{2,1,0:T(8,128)S(1)} %maximum_maximum_fusion.rest_0_), channel_id=1, source_target_pairs={{8,0},{0,8},{24,16},{16,24},{40,32},{32,40},{56,48},{48,56},{72,64... | collective-permute-start | bytes 1622024 | tf_op jit(solution)/shard_map/ppermute | solution.py:249
  1.3 15.1 %collective-permute-start.1 = (f32[2,264,256]{2,1,0:T(8,128)S(1)}, f32[2,264,256]{2,1,0:T(8,128)S(1)}, u32[]{:S(2)}, u32[]{:S(2)}) collective-permute-start(f32[2,264,256]{2,1,0:T(8,128)S(1)} %maximum_maximum_fusion.rest_0_), channel_id=1, source_target_pairs={{32,0},{40,8},{48,16},{56,24},{64,32},{72,40},{80,48},{88,56},{96,... | collective-permute-start | bytes 1622024 | tf_op jit(solution)/shard_map/ppermute | solution.py:249
  4.3 15.6 %collective-permute-start.2 = (f32[2,264,256]{2,1,0:T(8,128)S(1)}, f32[2,264,256]{2,1,0:T(8,128)S(1)}, u32[]{:S(2)}, u32[]{:S(2)}) collective-permute-start(f32[2,264,256]{2,1,0:T(8,128)S(1)} %maximum_maximum_fusion.rest_0_), channel_id=1, source_target_pairs={{96,0},{104,8},{112,16},{120,24},{0,32},{8,40},{16,48},{24,56},{32... | collective-permute-start | bytes 1622024 | tf_op jit(solution)/shard_map/ppermute | solution.py:249
  4.3 15.6 %collective-permute-start.3 = (f32[2,264,256]{2,1,0:T(8,128)S(1)}, f32[2,264,256]{2,1,0:T(8,128)S(1)}, u32[]{:S(2)}, u32[]{:S(2)}) collective-permute-start(f32[2,264,256]{2,1,0:T(8,128)S(1)} %maximum_maximum_fusion.rest_0_), channel_id=1, source_target_pairs={{16,0},{24,8},{0,16},{8,24},{48,32},{56,40},{32,48},{40,56},{80,64... | collective-permute-start | bytes 1622024 | tf_op jit(solution)/shard_map/ppermute | solution.py:249
  19.8 2.5 %collective-permute-start.7 = (f32[2,264,256]{2,1,0:T(8,128)S(1)}, f32[2,264,256]{2,1,0:T(8,128)S(1)}, u32[]{:S(2)}, u32[]{:S(2)}) collective-permute-start(f32[2,264,256]{2,1,0:T(8,128)S(1)} %collective-permute-done.1.rest_0_), channel_id=1, source_target_pairs={{8,0},{0,8},{24,16},{16,24},{40,32},{32,40},{56,48},{48,56},{72,64... | collective-permute-start | bytes 1622024 | tf_op jit(solution)/shard_map/ppermute | solution.py:249
  19.8 4.5 %collective-permute-start.8 = (f32[2,264,256]{2,1,0:T(8,128)S(1)}, f32[2,264,256]{2,1,0:T(8,128)S(1)}, u32[]{:S(2)}, u32[]{:S(2)}) collective-permute-start(f32[2,264,256]{2,1,0:T(8,128)S(1)} %collective-permute-done.2.rest_1_), channel_id=1, source_target_pairs={{8,0},{0,8},{24,16},{16,24},{40,32},{32,40},{56,48},{48,56},{72,64... | collective-permute-start | bytes 1622024 | tf_op jit(solution)/shard_map/ppermute | solution.py:249
  20.3 4.0 %collective-permute-start.9 = (f32[2,264,256]{2,1,0:T(8,128)S(1)}, f32[2,264,256]{2,1,0:T(8,128)S(1)}, u32[]{:S(2)}, u32[]{:S(2)}) collective-permute-start(f32[2,264,256]{2,1,0:T(8,128)S(1)} %collective-permute-done.3.rest_2_), channel_id=1, source_target_pairs={{8,0},{0,8},{24,16},{16,24},{40,32},{32,40},{56,48},{48,56},{72,64... | collective-permute-start | bytes 1622024 | tf_op jit(solution)/shard_map/ppermute | solution.py:249
  20.3 16.6 %collective-permute-start.4 = (f32[2,264,256]{2,1,0:T(8,128)S(1)}, f32[2,264,256]{2,1,0:T(8,128)S(1)}, u32[]{:S(2)}, u32[]{:S(2)}) collective-permute-start(f32[2,264,256]{2,1,0:T(8,128)S(1)} %collective-permute-done.1.rest_0_), channel_id=1, source_target_pairs={{32,0},{40,8},{48,16},{56,24},{64,32},{72,40},{80,48},{88,56},{96,... | collective-permute-start | bytes 1622024 | tf_op jit(solution)/shard_map/ppermute | solution.py:249
  22.2 15.6 %collective-permute-start.5 = (f32[2,264,256]{2,1,0:T(8,128)S(1)}, f32[2,264,256]{2,1,0:T(8,128)S(1)}, u32[]{:S(2)}, u32[]{:S(2)}) collective-permute-start(f32[2,264,256]{2,1,0:T(8,128)S(1)} %collective-permute-done.3.rest_2_), channel_id=1, source_target_pairs={{96,0},{104,8},{112,16},{120,24},{0,32},{8,40},{16,48},{24,56},{32... | collective-permute-start | bytes 1622024 | tf_op jit(solution)/shard_map/ppermute | solution.py:249
  22.4 15.5 %collective-permute-start.6 = (f32[2,264,256]{2,1,0:T(8,128)S(1)}, f32[2,264,256]{2,1,0:T(8,128)S(1)}, u32[]{:S(2)}, u32[]{:S(2)}) collective-permute-start(f32[2,264,256]{2,1,0:T(8,128)S(1)} %collective-permute-done.1.rest_0_), channel_id=1, source_target_pairs={{16,0},{24,8},{0,16},{8,24},{48,32},{56,40},{32,48},{40,56},{80,64... | collective-permute-start | bytes 1622024 | tf_op jit(solution)/shard_map/ppermute | solution.py:249
  24.3 1.1 %copy-start = (bf16[1536,256]{1,0:T(8,128)(2,1)S(1)}, bf16[1536,256]{1,0:T(8,128)(2,1)}, u32[]{:S(2)}) copy-start(bf16[1536,256]{1,0:T(8,128)(2,1)} %get-tuple-element.25.xh) | copy-start | bytes 2359300
  25.4 1.1 %copy-start.1 = (f8e4m3fn[1536,512]{1,0:T(32,128)(4,1)S(1)}, f8e4m3fn[1536,512]{1,0:T(32,128)(4,1)}, u32[]{:S(2)}) copy-start(f8e4m3fn[1536,512]{1,0:T(32,128)(4,1)} %get-tuple-element.26.x8) | copy-start | bytes 2359300
  37.9 13.3 %collective-permute-start.13 = (f32[2,264,256]{2,1,0:T(8,128)S(1)}, f32[2,264,256]{2,1,0:T(8,128)S(1)}, u32[]{:S(2)}, u32[]{:S(2)}) collective-permute-start(f32[2,264,256]{2,1,0:T(8,128)S(1)} %collective-permute-done.5.rest_1_), channel_id=1, source_target_pairs={{8,0},{0,8},{24,16},{16,24},{40,32},{32,40},{56,48},{48,56},{72,64... | collective-permute-start | bytes 1622024 | tf_op jit(solution)/shard_map/ppermute | solution.py:249
  38.0 13.2 %collective-permute-start.14 = (f32[2,264,256]{2,1,0:T(8,128)S(1)}, f32[2,264,256]{2,1,0:T(8,128)S(1)}, u32[]{:S(2)}, u32[]{:S(2)}) collective-permute-start(f32[2,264,256]{2,1,0:T(8,128)S(1)} %collective-permute-done.6.rest_2_), channel_id=1, source_target_pairs={{8,0},{0,8},{24,16},{16,24},{40,32},{32,40},{56,48},{48,56},{72,64... | collective-permute-start | bytes 1622024 | tf_op jit(solution)/shard_map/ppermute | solution.py:249
  38.6 8.5 %collective-permute-start.10 = (f32[1,264,256]{2,1,0:T(8,128)S(1)}, f32[1,264,256]{2,1,0:T(8,128)S(1)}, u32[]{:S(2)}, u32[]{:S(2)}) collective-permute-start(f32[1,264,256]{2,1,0:T(8,128)S(1)} %slice.6), channel_id=1, source_target_pairs={{32,0},{40,8},{48,16},{56,24},{64,32},{72,40},{80,48},{88,56},{96,... | collective-permute-start | bytes 811016 | tf_op jit(solution)/shard_map/ppermute | solution.py:249
  40.6 9.5 %collective-permute-start.11 = (f32[1,264,256]{2,1,0:T(8,128)S(1)}, f32[1,264,256]{2,1,0:T(8,128)}, u32[]{:S(2)}, u32[]{:S(2)}) collective-permute-start(f32[1,264,256]{2,1,0:T(8,128)S(1)} %slice.7), channel_id=1, source_target_pairs={{96,0},{104,8},{112,16},{120,24},{0,32},{8,40},{16,48},{24,56},{32... | collective-permute-start | bytes 811016 | tf_op jit(solution)/shard_map/ppermute | solution.py:249
  40.6 10.6 %collective-permute-start.12 = (f32[2,264,256]{2,1,0:T(8,128)S(1)}, f32[2,264,256]{2,1,0:T(8,128)S(1)}, u32[]{:S(2)}, u32[]{:S(2)}) collective-permute-start(f32[2,264,256]{2,1,0:T(8,128)S(1)} %collective-permute-done.4.rest_0_), channel_id=1, source_target_pairs={{8,0},{0,8},{24,16},{16,24},{40,32},{32,40},{56,48},{48,56},{72,64... | collective-permute-start | bytes 1622024 | tf_op jit(solution)/shard_map/ppermute | solution.py:249
  47.1 5.3 %copy-start.10 = (f32[1,264,256]{2,1,0:T(8,128)}, f32[1,264,256]{2,1,0:T(8,128)S(1)}, u32[]{:S(2)}) copy-start(f32[1,264,256]{2,1,0:T(8,128)S(1)} %collective-permute-done.10.rest_3_) | copy-start | bytes 811012
  50.1 2.0 %collective-permute-start.15 = (f32[1,264,256]{2,1,0:T(8,128)S(1)}, f32[1,264,256]{2,1,0:T(8,128)}, u32[]{:S(2)}, u32[]{:S(2)}) collective-permute-start(f32[1,264,256]{2,1,0:T(8,128)S(1)} %collective-permute-done.10.rest_3_), channel_id=1, source_target_pairs={{8,0},{0,8},{24,16},{16,24},{40,32},{32,40},{56,48},{48,56},{72,64... | collective-permute-start | bytes 811016 | tf_op jit(solution)/shard_map/ppermute | solution.py:249
  50.1 2.3 %collective-permute-start.16 = (f32[1,264,256]{2,1,0:T(8,128)}, f32[1,264,256]{2,1,0:T(8,128)}, u32[]{:S(2)}, u32[]{:S(2)}) collective-permute-start(f32[1,264,256]{2,1,0:T(8,128)} %collective-permute-done.11.rest_4_), channel_id=1, source_target_pairs={{8,0},{0,8},{24,16},{16,24},{40,32},{32,40},{56,48},{48,56},{72,64... | collective-permute-start | bytes 811016 | tf_op jit(solution)/shard_map/ppermute | solution.py:249
  51.2 1.2 %copy-start.8 = (f32[2,264,256]{2,1,0:T(8,128)}, f32[2,264,256]{2,1,0:T(8,128)S(1)}, u32[]{:S(2)}) copy-start(f32[2,264,256]{2,1,0:T(8,128)S(1)} %collective-permute-done.12.rest_0_) | copy-start | bytes 1622020
  51.2 1.2 %copy-start.6 = (f32[2,264,256]{2,1,0:T(8,128)}, f32[2,264,256]{2,1,0:T(8,128)S(1)}, u32[]{:S(2)}) copy-start(f32[2,264,256]{2,1,0:T(8,128)S(1)} %collective-permute-done.13.rest_1_) | copy-start | bytes 1622020
  51.3 1.1 %copy-start.7 = (f32[2,264,256]{2,1,0:T(8,128)}, f32[2,264,256]{2,1,0:T(8,128)S(1)}, u32[]{:S(2)}) copy-start(f32[2,264,256]{2,1,0:T(8,128)S(1)} %collective-permute-done.14.rest_2_) | copy-start | bytes 1622020
  (4 other events, 4.0 us)

commit v2 on v1

v2 whole, which is shorter than its diff:
```python
import functools
import math

import jax
import jax.numpy as jnp
from jax import lax
from jax.experimental import pallas as pl
from jax.experimental.pallas import tpu as pltpu
from jax.sharding import PartitionSpec as P

F32, BF16, F8 = jnp.float32, jnp.bfloat16, jnp.float8_e4m3fn
LOG2E = 1.4426950408889634
UNIT = 256
PACKED = 264
LIFT = 256.0
GRANT = 35 << 20
ROWS = 256
VMEM = pl.BlockSpec(memory_space=pltpu.VMEM)
ANY = pl.BlockSpec(memory_space=pl.ANY)
HBM = pl.BlockSpec(memory_space=pltpu.HBM)


def constants(width):
    scale = LOG2E / math.sqrt(width)
    return scale, 0.5 * LOG2E * math.sqrt(width)


def prepare_points(x_ref, xh_ref, x8_ref, a_ref):
    scale, offset = constants(x_ref.shape[1])
    for q in range(0, x_ref.shape[0], ROWS):
        r = slice(q, q + ROWS)
        x = x_ref[r, :]
        high = x.astype(BF16)
        low = (x - high.astype(F32)) * LIFT
        xh_ref[r, :] = high
        x8_ref[r, :] = jnp.concatenate([x.astype(F8), low.astype(F8)], axis=1)
        a = jnp.sum(x * x, axis=1, keepdims=True) * (-0.5 * scale) + offset
        a_ref[r, :] = jnp.broadcast_to(a, (ROWS, 128))


def prepare_units(refs, wh_ref, w8_ref, b_ref, c_ref):
    i = 0
    for ref in refs:
        for j in range(ref.shape[0]):
            width = ref.shape[2]
            scale, offset = constants(width)
            t = ref[j, 0:UNIT, :].T
            scaled = t * scale
            high = scaled.astype(BF16)
            low = (scaled - high.astype(F32)) * (LIFT / scale)
            wh_ref[i] = high
            w8_ref[i] = jnp.concatenate([low.astype(F8), t.astype(F8)], axis=0)
            b_ref[i] = jnp.sum(t * t, axis=0, keepdims=True) * (-0.5 * scale) + offset
            c_ref[i] = ref[j, UNIT : UNIT + 1, :]
            i += 1


def tile(i, r, xh_ref, x8_ref, a_ref, wh_ref, w8_ref, b_ref, c_ref, k_ref):
    scale, _ = constants(xh_ref.shape[1])
    main = jnp.dot(xh_ref[r, :], wh_ref[i], preferred_element_type=F32)
    cross = jnp.dot(x8_ref[r, :], w8_ref[i], preferred_element_type=F32)
    a = a_ref[r, :]
    value = None
    for t in range(0, UNIT, 128):
        c = slice(t, t + 128)
        k = jnp.exp2(main[:, c] + cross[:, c] * (scale / LIFT) + a + b_ref[i, :, c])
        k_ref[i, r, c] = k
        term = k * c_ref[i, :, c]
        value = term if value is None else value + term
    return value


def first_product(group, points, prepared, v_in, v_ref, k_ref, saved=None, sem=None):
    units = k_ref.shape[0]
    assert units % group == 0

    def save(j, q):
        part = (pl.ds(j * group, group), pl.ds(q, ROWS))
        return pltpu.make_async_copy(k_ref.at[part], saved.at[part], sem)

    @pl.loop(0, units // group)
    def _(j):
        for q in range(0, points[0].shape[0], ROWS):
            r = slice(q, q + ROWS)
            value = None
            for u in range(group):
                term = tile(j * group + u, r, *points, *prepared, k_ref)
                value = term if value is None else value + term
            before = 0.0 if v_in is None else v_in[r, :]
            v_ref[r, :] = jnp.where(j == 0, before, v_ref[r, :]) + value
            if saved is not None:
                save(j, q).start()

    if saved is not None:
        pltpu.make_async_copy(k_ref, saved, sem).wait()


def opening_kernel(group, x_ref, *rest):
    units, (xh, x8, a, v, k), prepared = rest[:2], rest[2:7], rest[7:]
    prepare_points(x_ref, xh, x8, a)
    prepare_units(units, *prepared)
    v[...] = jnp.zeros_like(v)
    first_product(group, (xh, x8, a), prepared, None, v, k)


def load(sources, targets, sem):
    copies = [pltpu.make_async_copy(f, t, sem.at[i]) for i, (f, t) in enumerate(zip(sources, targets))]
    for copy in copies:
        copy.start()
    return copies


def middle_kernel(n, group, *rest):
    sources, units, (v, saved), scratch = rest[:4], rest[4 : 4 + n], rest[4 + n : 6 + n], rest[6 + n :]
    (xh, x8, a, v_in), prepared, sem = scratch[:4], scratch[4:8], scratch[8]
    copies = load(sources, scratch[:4], sem)
    prepare_units(units, *prepared)
    for copy in copies:
        copy.wait()
    v[...] = v_in[...]
    if len(scratch) > 9:
        k, save_sem = scratch[9:]
        first_product(group, (xh, x8, a), prepared, v_in, v, k, saved, save_sem)
    else:
        first_product(group, (xh, x8, a), prepared, v_in, v, saved)


def closing_kernel(n, m, f, group, place_ref, *rest):
    sources, units, kept, saved = rest[:4], rest[4 : 4 + n], rest[4 + n : 4 + n + m], rest[4 + n + m : 4 + n + m + f]
    out, xh, x8, a, v_in, v, sums, k, *prepared, held, points_sem, sem = rest[4 + n + m + f :]
    copies = load(sources, (xh, x8, a, v_in), points_sem)
    (saved,) = saved
    early = held.shape[0]
    late = saved.shape[0] - early
    fetch = pltpu.make_async_copy(saved.at[0:early], held, sem.at[0])
    fetch_late = pltpu.make_async_copy(saved.at[early:], k.at[0:late], sem.at[1])
    prepare_units(units, *prepared)
    for copy in copies:
        copy.wait()
    fetch.start()
    v[...] = v_in[...]
    first_product(group, (xh, x8, a), prepared, v_in, v, k)
    for q in range(0, v.shape[0], ROWS):
        r = slice(q, q + ROWS)
        v[r, :] = jnp.broadcast_to(jnp.sum(v[r, :], axis=1, keepdims=True), (ROWS, 128))
    second_product(k, v, sums, 0)
    fetch_late.start()
    at = k.shape[0]
    for part in kept:
        second_product(part, v, sums, at)
        at += part.shape[0]
    fetch.wait()
    second_product(held, v, sums, at)
    fetch_late.wait()
    second_product(k.at[0:late], v, sums, at + early)
    for i in range(place_ref.shape[0]):
        for h in range(2):
            row = sums[2 * i + h]
            for j in range(out.shape[1]):
                out[place_ref[i], j, :, h * UNIT : (h + 1) * UNIT] = row


def second_product(k_ref, v_ref, sums, at):
    units, rows = k_ref.shape[:2]
    group = next(g for g in (5, 4, 3, 2, 1) if units % g == 0)
    lanes = [slice(t, t + 128) for t in range(0, UNIT, 128)]

    @pl.loop(0, units // group)
    def _(j):
        total = {}
        for q in range(0, rows, 8):
            v = v_ref[q : q + 8, :]
            for u in range(group):
                for t, c in enumerate(lanes):
                    term = k_ref[j * group + u, q : q + 8, c] * v
                    total[u, t] = total[u, t] + term if q else term
        for u in range(group):
            for t, c in enumerate(lanes):
                sums[at + j * group + u, :, c] = jnp.sum(total[u, t], axis=0, keepdims=True)


def points_scratch(rows, width):
    return [pltpu.VMEM(s, d) for s, d in (((rows, width), BF16), ((rows, 2 * width), F8), ((rows, 128), F32), ((rows, 128), F32))]


def prepared_scratch(n, width):
    return [
        pltpu.VMEM((n, width, UNIT), BF16),
        pltpu.VMEM((n, 2 * width, UNIT), F8),
        pltpu.VMEM((n, 1, UNIT), F32),
        pltpu.VMEM((n, 1, UNIT), F32),
    ]


def cost(rows, n, width):
    return pl.CostEstimate(
        flops=8 * rows * n * UNIT * width, bytes_accessed=rows * n * UNIT * 4, transcendentals=rows * n * UNIT
    )


def of(shape, dtype=F32):
    return jax.ShapeDtypeStruct(shape, dtype)


def count(blocks):
    return sum(b.shape[0] for b in blocks)


def opening(group, x, blocks):
    rows, width = x.shape
    n = count(blocks)
    return pl.pallas_call(
        functools.partial(opening_kernel, group),
        in_specs=[VMEM] * 3,
        out_specs=[VMEM] * 5,
        out_shape=[of((rows, width), BF16), of((rows, 2 * width), F8), of((rows, 128)), of((rows, 128)), pltpu.VMEM((n, rows, UNIT), F32)],
        scratch_shapes=prepared_scratch(n, width),
        cost_estimate=cost(rows, n, width),
        compiler_params=pltpu.CompilerParams(vmem_limit_bytes=GRANT),
        name="opening",
    )(x, *blocks)


def middle(group, xh, x8, a, v, blocks, keep):
    rows, width = xh.shape
    n = count(blocks)
    return pl.pallas_call(
        functools.partial(middle_kernel, len(blocks), group),
        in_specs=[ANY] * 4 + [VMEM] * len(blocks),
        out_specs=[VMEM, VMEM if keep else HBM],
        out_shape=[of((rows, 128)), (pltpu.VMEM((n, rows, UNIT), F32) if keep else of((n, rows, UNIT)))],
        scratch_shapes=[
            *points_scratch(rows, width),
            *prepared_scratch(n, width),
            pltpu.SemaphoreType.DMA((4,)),
            *([] if keep else [pltpu.VMEM((n, rows, UNIT), F32), pltpu.SemaphoreType.DMA]),
        ],
        cost_estimate=cost(rows, n, width),
        compiler_params=pltpu.CompilerParams(vmem_limit_bytes=GRANT),
        name="middle",
    )(xh, x8, a, v, *blocks)


def closing(group, early, place, copies, xh, x8, a, v, blocks, kept, saved):
    rows, width = xh.shape
    n = count(blocks)
    total = n + count(kept) + count(saved)
    return pl.pallas_call(
        functools.partial(closing_kernel, len(blocks), len(kept), len(saved), group),
        in_specs=[pl.BlockSpec(memory_space=pltpu.SMEM)] + [ANY] * 4 + [VMEM] * (len(blocks) + len(kept)) + [HBM] * len(saved),
        out_specs=VMEM,
        out_shape=of((total // 2, copies, 1, 2 * UNIT)),
        scratch_shapes=[
            *points_scratch(rows, width),
            pltpu.VMEM((rows, 128), F32),
            pltpu.VMEM((total, 1, UNIT), F32),
            pltpu.VMEM((n, rows, UNIT), F32),
            *prepared_scratch(n, width),
            pltpu.VMEM((early, rows, UNIT), F32),
            pltpu.SemaphoreType.DMA((4,)),
            pltpu.SemaphoreType.DMA((2,)),
        ],
        cost_estimate=cost(rows, 2 * n, width),
        compiler_params=pltpu.CompilerParams(vmem_limit_bytes=GRANT),
        name="closing",
    )(place, xh, x8, a, v, *blocks, *[pltpu.with_memory_space_constraint(k, pltpu.VMEM) for k in kept], *saved)


RING, PAIR, CORES = 4, 2, 2


def index(x, z, core):
    return ((x % RING) * PAIR + z % PAIR) * CORES + core % CORES


def fetch(array, x=0, z=0, core=0):
    pairs = [
        (index(i + x, j + z, k + core), index(i, j, k))
        for i in range(RING)
        for j in range(PAIR)
        for k in range(CORES)
    ]
    return lax.ppermute(array, "blk", pairs)


def body(points, centres, coefficients):
    rows_size = lax.axis_size("rows")
    width = centres.shape[1]
    total_points = points.shape[0] * lax.axis_size("blk") * rows_size
    units = centres.shape[0] // UNIT
    own = jnp.concatenate(
        [
            centres.reshape(units, UNIT, width),
            coefficients.reshape(units, 1, UNIT),
            jnp.zeros((units, PACKED - UNIT - 1, width), F32),
        ],
        axis=1,
    )
    me = lax.axis_index("blk")
    at_x, at_z, at_core = me // (PAIR * CORES), me // CORES % PAIR, me % CORES

    def place(x, z, core):
        return index(at_x + x, at_z + z, at_core + core)

    def other(array):
        return fetch(array, core=1)

    order = [(2, 0, 1), (-1, 1, 1), (1, 1, 1), (2, 1, 0), (2, 1, 1)]
    order += [(0, 0, 0), (0, 0, 1)]
    order += [(2, 0, 0), (-1, 1, 0), (1, 1, 0)]
    order += [(1, 0, 0), (-1, 0, 0), (0, 1, 0), (1, 0, 1), (-1, 0, 1), (0, 1, 1)]
    places = jnp.stack([place(*o) for o in order]).astype(jnp.int32)
    after = lax.optimization_barrier
    near = [fetch(own, x=1), fetch(own, x=-1), fetch(own, z=1)]
    beside = other(own)
    xh, x8, a, v, k0 = opening(2, points, [own, beside])
    *near, v, places = after((*near, v, places))
    up, down, across = near
    far = [fetch(up, x=1), fetch(across, x=-1), fetch(up, z=1)]
    near_other = [other(b) for b in near]
    v, k1 = middle(4, xh, x8, a, v, near + near_other, False)
    *far, v = after((*far, v))
    last = [fetch(far[2][0:1], x=1), fetch(far[1][1:2], x=-1)]
    far_other = [other(b) for b in far]
    v, k2 = middle(3, xh, x8, a, v, far, True)
    *last, v = after((*last, v))
    last_other = [other(b) for b in last]
    sums = closing(10, 8, places, rows_size, xh, x8, a, v, far_other + last + last_other, [k0, k2], [k1])
    parts = lax.all_to_all(sums.reshape(-1, 1, 2 * UNIT), ("blk", "rows"), 0, 0, tiled=True)
    return jnp.sum(parts, axis=(0, 1)) / total_points


def solution(mesh):
    return jax.shard_map(
        body,
        mesh=mesh,
        in_specs=(P(("blk", "rows"), None), P("blk", None), P("blk")),
        out_specs=P("blk"),
        check_vma=False,
    )
```

time: 89 us -> 85.9 us (0.965)
  waiting for transfers between devices: 11.6 us -> 19.8 us
  Pallas kernels: 35.6 us -> 28.8 us
  local copies, waits for them, and re-layouts: 6.96 us -> 2.5 us
    ppermute x17, waiting for transfers between devices: 11.6 us -> 19.8 us  [fetch(): return lax.ppermute(array, 'blk', pairs)]
    pallas_call x2, Pallas kernels: 22.8 us -> 16.5 us  [the longest x1 13.4 us: closing(): pl.pallas_call(functools.partial(closing_kernel, len(blocks), len(kept),...]
    unnamed x22 -> x8, local copies, waits for them, and re-layouts: 6.24 us -> 2.29 us
  transfers between devices with their start and end apart: 17 -> 17, of which waited for: 7 -> 8; matrix products, arithmetic and copies ran while one was open for 1% -> 0% of each run, Pallas kernels for 23% -> 18%
where the time goes in v2:
time: 85.9 us; the launch traced here: 84.7 us
  Pallas kernels  28.8 us (34%)
  waiting for transfers between devices  19.8 us (23%)
  blocking collectives  18.8 us (22%)
  starting transfers between devices  12.6 us (15%)
  local copies, waits for them, and re-layouts  2.5 us (3%)
  other arithmetic  1.95 us (2%)
    ppermute x17, waiting for transfers between devices, fetch(): return lax.ppermute(array, 'blk', pairs)  19.8 us
    all_to_all x1, blocking collectives, body(): lax.all_to_all(sums.reshape(-1, 1, 2 * UNIT), ('blk', 'rows'), 0, 0, tile...  18.8 us
    pallas_call x1, Pallas kernels, closing(): pl.pallas_call(functools.partial(closing_kernel, len(blocks), len(kept),...  13.4 us
    ppermute x17, starting transfers between devices, fetch(): return lax.ppermute(array, 'blk', pairs)  12.6 us
    pallas_call x2, Pallas kernels, middle(): pl.pallas_call(functools.partial(middle_kernel, len(blocks), group), in_s...  12.3 us
    pallas_call x1, Pallas kernels, opening(): pl.pallas_call(functools.partial(opening_kernel, group), in_specs=[VMEM]...  3.13 us
    unnamed x8, local copies, waits for them, and re-layouts  2.29 us
  transfers between devices with their start and end apart: 17, of which 8 were waited for; matrix products, arithmetic and copies ran while one was open for 0% of the time, Pallas kernels for 18%

profile of v2, /device:TPU:0, one launch (start us, length us, event | category | flops | bytes accessed | tf_op | source)
XLA Modules:
  0.0 84.7 jit_solution(3996066076104449048)
XLA Ops:
  0.1 1.2 %maximum_maximum_fusion.rest_0_ = f32[2,264,256]{2,1,0:T(8,128)S(1)} fusion(f32[2,1,256]{2,1,0:T(1,128)} %bitcast.21, f32[2,256,256]{2,1,0:T(8,128)} %bitcast.20, f32[264]{0:T(512)S(1)} %pad.2.clone), kind=kLoop, calls=%fused_computation | loop fusion | flops 270336 | bytes 1068064 | tf_op jit(solution)/shard_map/concatenate | solution.py:291
  1.3 2.9 %collective-permute-start = (f32[2,264,256]{2,1,0:T(8,128)S(1)}, f32[2,264,256]{2,1,0:T(8,128)S(1)}, u32[]{:S(2)}, u32[]{:S(2)}) collective-permute-start(f32[2,264,256]{2,1,0:T(8,128)S(1)} %maximum_maximum_fusion.rest_0_), channel_id=1, source_target_pairs={{32,0},{40,8},{48,16},{56,24},{64,32},{72,40},{80,48},{88,56},{96,... | collective-permute-start | bytes 1622024 | tf_op jit(solution)/shard_map/ppermute | solution.py:283
  4.3 1.9 %collective-permute-start.2 = (f32[2,264,256]{2,1,0:T(8,128)S(1)}, f32[2,264,256]{2,1,0:T(8,128)S(1)}, u32[]{:S(2)}, u32[]{:S(2)}) collective-permute-start(f32[2,264,256]{2,1,0:T(8,128)S(1)} %maximum_maximum_fusion.rest_0_), channel_id=1, source_target_pairs={{16,0},{24,8},{0,16},{8,24},{48,32},{56,40},{32,48},{40,56},{80,64... | collective-permute-start | bytes 1622024 | tf_op jit(solution)/shard_map/ppermute | solution.py:283
  6.3 1.4 %copy-done = f32[1536,256]{1,0:T(8,128)S(1)} copy-done((f32[1536,256]{1,0:T(8,128)S(1)}, f32[1536,256]{1,0:T(8,128)}, u32[]{:S(2)}) %copy-start) | copy-done | bytes 1572888
  7.7 3.1 %opening.1 = (bf16[1536,256]{1,0:T(8,128)(2,1)S(1)}, f8e4m3fn[1536,512]{1,0:T(32,128)(4,1)S(1)}, f32[1536,128]{1,0:T(8,128)S(1)}, f32[1536,128]{1,0:T(8,128)S(1)}, f32[4,1536,256]{2,1,0:T(8,128)S(1)}) custom-call(f32[1536,256]{1,0:T(8,128)S(1)} %copy-done, f32[2,264,256]{2,1,0:T(8,128)S(1)} %maximum_maximum_fusion.rest_0_, ...), custom_call_target="tpu_custom_call" | custom-call | flops 3221225472 | bytes 6291456 | tf_op jit(solution)/shard_map/opening/pallas_call | solution.py:212
  10.8 5.5 %collective-permute-done.rest_4_ = f32[2,264,256]{2,1,0:T(8,128)S(1)} collective-permute-done((f32[2,264,256]{2,1,0:T(8,128)S(1)}, f32[2,264,256]{2,1,0:T(8,128)S(1)}, u32[]{:S(2)}, u32[]{:S(2)}) %collective-permute-start) | collective-permute-done | bytes 540704 | tf_op jit(solution)/shard_map/ppermute | solution.py:283
  16.4 3.4 %collective-permute-done.1.rest_5_ = f32[2,264,256]{2,1,0:T(8,128)S(1)} collective-permute-done((f32[2,264,256]{2,1,0:T(8,128)S(1)}, f32[2,264,256]{2,1,0:T(8,128)S(1)}, u32[]{:S(2)}, u32[]{:S(2)}) %collective-permute-start.1) | collective-permute-done | bytes 540704 | tf_op jit(solution)/shard_map/ppermute | solution.py:283
  19.8 0.5 collective-permute-start.8
  20.3 1.9 %collective-permute-start.4 = (f32[2,264,256]{2,1,0:T(8,128)S(1)}, f32[2,264,256]{2,1,0:T(8,128)S(1)}, u32[]{:S(2)}, u32[]{:S(2)}) collective-permute-start(f32[2,264,256]{2,1,0:T(8,128)S(1)} %collective-permute-done.rest_4_), channel_id=1, source_target_pairs={{32,0},{40,8},{48,16},{56,24},{64,32},{72,40},{80,48},{88,56},{96,... | collective-permute-start | bytes 1622024 | tf_op jit(solution)/shard_map/ppermute | solution.py:283
  22.4 1.9 %collective-permute-start.6 = (f32[2,264,256]{2,1,0:T(8,128)S(1)}, f32[2,264,256]{2,1,0:T(8,128)S(1)}, u32[]{:S(2)}, u32[]{:S(2)}) collective-permute-start(f32[2,264,256]{2,1,0:T(8,128)S(1)} %collective-permute-done.rest_4_), channel_id=1, source_target_pairs={{16,0},{24,8},{0,16},{8,24},{48,32},{56,40},{32,48},{40,56},{80,64... | collective-permute-start | bytes 1622024 | tf_op jit(solution)/shard_map/ppermute | solution.py:283
  24.3 8.3 %middle.2 = (f32[1536,128]{1,0:T(8,128)S(1)}, f32[12,1536,256]{2,1,0:T(8,128)}) custom-call(bf16[1536,256]{1,0:T(8,128)(2,1)S(1)} %get-tuple-element.28.rest_0_, f8e4m3fn[1536,512]{1,0:T(32,128)(4,1)S(1)} %get-tuple-element.29.rest_1_, f32[1536,128]{1,0:T(8,128)S(1)} %get-tuple-element.30.rest_2_, f32[1536,128]{1,0:T(8,128)S(1)} %get-tuple-element.33.rest_3_, ...), custom_call_target="tpu_custom_call" | custom-call | flops 9663676416 | bytes 18874368 | tf_op jit(solution)/shard_map/middle/pallas_call | solution.py:227
  32.6 2.4 %collective-permute-done.4.rest_4_ = f32[2,264,256]{2,1,0:T(8,128)S(1)} collective-permute-done((f32[2,264,256]{2,1,0:T(8,128)S(1)}, f32[2,264,256]{2,1,0:T(8,128)S(1)}, u32[]{:S(2)}, u32[]{:S(2)}) %collective-permute-start.4) | collective-permute-done | bytes 540704 | tf_op jit(solution)/shard_map/ppermute | solution.py:283
  35.0 2.8 %collective-permute-done.5.rest_5_ = f32[2,264,256]{2,1,0:T(8,128)S(1)} collective-permute-done((f32[2,264,256]{2,1,0:T(8,128)S(1)}, f32[2,264,256]{2,1,0:T(8,128)S(1)}, u32[]{:S(2)}, u32[]{:S(2)}) %collective-permute-start.5) | collective-permute-done | bytes 540704 | tf_op jit(solution)/shard_map/ppermute | solution.py:283
  38.0 0.6 collective-permute-start.14
  38.6 1.7 %collective-permute-start.10 = (f32[1,264,256]{2,1,0:T(8,128)S(1)}, f32[1,264,256]{2,1,0:T(8,128)S(1)}, u32[]{:S(2)}, u32[]{:S(2)}) collective-permute-start(f32[1,264,256]{2,1,0:T(8,128)S(1)} %slice.6), channel_id=1, source_target_pairs={{32,0},{40,8},{48,16},{56,24},{64,32},{72,40},{80,48},{88,56},{96,... | collective-permute-start | bytes 811016 | tf_op jit(solution)/shard_map/ppermute | solution.py:283
  40.6 4.0 %middle.3 = (f32[1536,128]{1,0:T(8,128)S(1)}, f32[6,1536,256]{2,1,0:T(8,128)S(1)}) custom-call(bf16[1536,256]{1,0:T(8,128)(2,1)S(1)} %get-tuple-element.28.rest_0_, f8e4m3fn[1536,512]{1,0:T(32,128)(4,1)S(1)} %get-tuple-element.29.rest_1_, f32[1536,128]{1,0:T(8,128)S(1)} %get-tuple-element.30.rest_2_, f32[1536,128]{1,0:T(8,128)S(1)} %get-tuple-element.38.rest_3_, ...), custom_call_target="tpu_custom_call" | custom-call | flops 4831838208 | bytes 9437184 | tf_op jit(solution)/shard_map/middle/pallas_call | solution.py:227
  44.6 0.9 %copy-done.3 = f32[1536,128]{1,0:T(8,128)} copy-done((f32[1536,128]{1,0:T(8,128)}, f32[1536,128]{1,0:T(8,128)S(1)}, u32[]{:S(2)}) %copy-start.3) | copy-done | bytes 786456
  45.5 1.5 %collective-permute-done.10.rest_7_ = f32[1,264,256]{2,1,0:T(8,128)S(1)} collective-permute-done((f32[1,264,256]{2,1,0:T(8,128)S(1)}, f32[1,264,256]{2,1,0:T(8,128)S(1)}, u32[]{:S(2)}, u32[]{:S(2)}) %collective-permute-start.10) | collective-permute-done | bytes 270368 | tf_op jit(solution)/shard_map/ppermute | solution.py:283
  47.0 2.7 %collective-permute-done.11.rest_8_ = f32[1,264,256]{2,1,0:T(8,128)S(1)} collective-permute-done((f32[1,264,256]{2,1,0:T(8,128)S(1)}, f32[1,264,256]{2,1,0:T(8,128)S(1)}, u32[]{:S(2)}, u32[]{:S(2)}) %collective-permute-start.11) | collective-permute-done | bytes 270368 | tf_op jit(solution)/shard_map/ppermute | solution.py:283
  49.7 0.5 collective-permute-start.16
  50.2 1.0 %collective-permute-done.15.rest_9_ = f32[1,264,256]{2,1,0:T(8,128)S(1)} collective-permute-done((f32[1,264,256]{2,1,0:T(8,128)S(1)}, f32[1,264,256]{2,1,0:T(8,128)S(1)}, u32[]{:S(2)}, u32[]{:S(2)}) %collective-permute-start.15) | collective-permute-done | bytes 270368 | tf_op jit(solution)/shard_map/ppermute | solution.py:283
  51.7 13.4 %closing.1 = f32[16,8,1,512]{3,2,1,0:T(1,128)S(1)} custom-call(s32[16]{0:T(128)S(1)} %stack.67.place_ref, bf16[1536,256]{1,0:T(8,128)(2,1)S(1)} %get-tuple-element.28.rest_0_, f8e4m3fn[1536,512]{1,0:T(32,128)(4,1)} %copy-done.1, f32[1536,128]{1,0:T(8,128)} %copy-done.2, f32[1536,128]{1,0:T(8,128)} %copy-done.3, ...), custom_call_target="tpu_custom_call" | custom-call | flops 16106127360 | bytes 31457280 | tf_op jit(solution)/shard_map/closing/pallas_call | solution.py:248
  65.0 18.8 %all_to_all.5 = f32[128,1,512]{2,1,0:T(1,128)S(1)} all-to-all(f32[128,1,512]{2,1,0:T(1,128)S(1)} %bitcast.19), channel_id=1, replica_groups=mesh['blk'=16,'rows'=8] {'blk','rows'}, dimensions={0} | all-to-all | bytes 524288 | tf_op jit(solution)/shard_map/all_to_all | solution.py:329
  84.1 0.6 broadcast_multiply_fusion
  (31 shorter events, 1.4 us)
Async XLA Ops:
  1.2 5.0 %collective-permute-start.3 = (f32[2,264,256]{2,1,0:T(8,128)S(1)}, f32[2,264,256]{2,1,0:T(8,128)S(1)}, u32[]{:S(2)}, u32[]{:S(2)}) collective-permute-start(f32[2,264,256]{2,1,0:T(8,128)S(1)} %maximum_maximum_fusion.rest_0_), channel_id=1, source_target_pairs={{8,0},{0,8},{24,16},{16,24},{40,32},{32,40},{56,48},{48,56},{72,64... | collective-permute-start | bytes 1622024 | tf_op jit(solution)/shard_map/ppermute | solution.py:283
  1.3 15.1 %collective-permute-start = (f32[2,264,256]{2,1,0:T(8,128)S(1)}, f32[2,264,256]{2,1,0:T(8,128)S(1)}, u32[]{:S(2)}, u32[]{:S(2)}) collective-permute-start(f32[2,264,256]{2,1,0:T(8,128)S(1)} %maximum_maximum_fusion.rest_0_), channel_id=1, source_target_pairs={{32,0},{40,8},{48,16},{56,24},{64,32},{72,40},{80,48},{88,56},{96,... | collective-permute-start | bytes 1622024 | tf_op jit(solution)/shard_map/ppermute | solution.py:283
  4.2 15.6 %collective-permute-start.1 = (f32[2,264,256]{2,1,0:T(8,128)S(1)}, f32[2,264,256]{2,1,0:T(8,128)S(1)}, u32[]{:S(2)}, u32[]{:S(2)}) collective-permute-start(f32[2,264,256]{2,1,0:T(8,128)S(1)} %maximum_maximum_fusion.rest_0_), channel_id=1, source_target_pairs={{96,0},{104,8},{112,16},{120,24},{0,32},{8,40},{16,48},{24,56},{32... | collective-permute-start | bytes 1622024 | tf_op jit(solution)/shard_map/ppermute | solution.py:283
  4.3 15.6 %collective-permute-start.2 = (f32[2,264,256]{2,1,0:T(8,128)S(1)}, f32[2,264,256]{2,1,0:T(8,128)S(1)}, u32[]{:S(2)}, u32[]{:S(2)}) collective-permute-start(f32[2,264,256]{2,1,0:T(8,128)S(1)} %maximum_maximum_fusion.rest_0_), channel_id=1, source_target_pairs={{16,0},{24,8},{0,16},{8,24},{48,32},{56,40},{32,48},{40,56},{80,64... | collective-permute-start | bytes 1622024 | tf_op jit(solution)/shard_map/ppermute | solution.py:283
  6.3 1.4 %copy-start = (f32[1536,256]{1,0:T(8,128)S(1)}, f32[1536,256]{1,0:T(8,128)}, u32[]{:S(2)}) copy-start(f32[1536,256]{1,0:T(8,128)} %x_ref.1) | copy-start | bytes 4718596
  10.8 29.8 %copy-start.1 = (f8e4m3fn[1536,512]{1,0:T(32,128)(4,1)}, f8e4m3fn[1536,512]{1,0:T(32,128)(4,1)S(1)}, u32[]{:S(2)}) copy-start(f8e4m3fn[1536,512]{1,0:T(32,128)(4,1)S(1)} %get-tuple-element.29.rest_1_) | copy-start | bytes 2359300
  10.8 29.8 %copy-start.2 = (f32[1536,128]{1,0:T(8,128)}, f32[1536,128]{1,0:T(8,128)S(1)}, u32[]{:S(2)}) copy-start(f32[1536,128]{1,0:T(8,128)S(1)} %get-tuple-element.30.rest_2_) | copy-start | bytes 2359300
  19.8 2.5 %collective-permute-start.7 = (f32[2,264,256]{2,1,0:T(8,128)S(1)}, f32[2,264,256]{2,1,0:T(8,128)S(1)}, u32[]{:S(2)}, u32[]{:S(2)}) collective-permute-start(f32[2,264,256]{2,1,0:T(8,128)S(1)} %collective-permute-done.rest_4_), channel_id=1, source_target_pairs={{8,0},{0,8},{24,16},{16,24},{40,32},{32,40},{56,48},{48,56},{72,64... | collective-permute-start | bytes 1622024 | tf_op jit(solution)/shard_map/ppermute | solution.py:283
  19.8 4.5 %collective-permute-start.8 = (f32[2,264,256]{2,1,0:T(8,128)S(1)}, f32[2,264,256]{2,1,0:T(8,128)S(1)}, u32[]{:S(2)}, u32[]{:S(2)}) collective-permute-start(f32[2,264,256]{2,1,0:T(8,128)S(1)} %collective-permute-done.1.rest_5_), channel_id=1, source_target_pairs={{8,0},{0,8},{24,16},{16,24},{40,32},{32,40},{56,48},{48,56},{72,64... | collective-permute-start | bytes 1622024 | tf_op jit(solution)/shard_map/ppermute | solution.py:283
  20.3 4.0 %collective-permute-start.9 = (f32[2,264,256]{2,1,0:T(8,128)S(1)}, f32[2,264,256]{2,1,0:T(8,128)S(1)}, u32[]{:S(2)}, u32[]{:S(2)}) collective-permute-start(f32[2,264,256]{2,1,0:T(8,128)S(1)} %collective-permute-done.2.rest_6_), channel_id=1, source_target_pairs={{8,0},{0,8},{24,16},{16,24},{40,32},{32,40},{56,48},{48,56},{72,64... | collective-permute-start | bytes 1622024 | tf_op jit(solution)/shard_map/ppermute | solution.py:283
  20.3 14.7 %collective-permute-start.4 = (f32[2,264,256]{2,1,0:T(8,128)S(1)}, f32[2,264,256]{2,1,0:T(8,128)S(1)}, u32[]{:S(2)}, u32[]{:S(2)}) collective-permute-start(f32[2,264,256]{2,1,0:T(8,128)S(1)} %collective-permute-done.rest_4_), channel_id=1, source_target_pairs={{32,0},{40,8},{48,16},{56,24},{64,32},{72,40},{80,48},{88,56},{96,... | collective-permute-start | bytes 1622024 | tf_op jit(solution)/shard_map/ppermute | solution.py:283
  22.2 15.6 %collective-permute-start.5 = (f32[2,264,256]{2,1,0:T(8,128)S(1)}, f32[2,264,256]{2,1,0:T(8,128)S(1)}, u32[]{:S(2)}, u32[]{:S(2)}) collective-permute-start(f32[2,264,256]{2,1,0:T(8,128)S(1)} %collective-permute-done.2.rest_6_), channel_id=1, source_target_pairs={{96,0},{104,8},{112,16},{120,24},{0,32},{8,40},{16,48},{24,56},{32... | collective-permute-start | bytes 1622024 | tf_op jit(solution)/shard_map/ppermute | solution.py:283
  22.4 15.5 %collective-permute-start.6 = (f32[2,264,256]{2,1,0:T(8,128)S(1)}, f32[2,264,256]{2,1,0:T(8,128)S(1)}, u32[]{:S(2)}, u32[]{:S(2)}) collective-permute-start(f32[2,264,256]{2,1,0:T(8,128)S(1)} %collective-permute-done.rest_4_), channel_id=1, source_target_pairs={{16,0},{24,8},{0,16},{8,24},{48,32},{56,40},{32,48},{40,56},{80,64... | collective-permute-start | bytes 1622024 | tf_op jit(solution)/shard_map/ppermute | solution.py:283
  37.9 12.4 %collective-permute-start.13 = (f32[2,264,256]{2,1,0:T(8,128)S(1)}, f32[2,264,256]{2,1,0:T(8,128)S(1)}, u32[]{:S(2)}, u32[]{:S(2)}) collective-permute-start(f32[2,264,256]{2,1,0:T(8,128)S(1)} %collective-permute-done.5.rest_5_), channel_id=1, source_target_pairs={{8,0},{0,8},{24,16},{16,24},{40,32},{32,40},{56,48},{48,56},{72,64... | collective-permute-start | bytes 1622024 | tf_op jit(solution)/shard_map/ppermute | solution.py:283
  38.0 12.2 %collective-permute-start.14 = (f32[2,264,256]{2,1,0:T(8,128)S(1)}, f32[2,264,256]{2,1,0:T(8,128)S(1)}, u32[]{:S(2)}, u32[]{:S(2)}) collective-permute-start(f32[2,264,256]{2,1,0:T(8,128)S(1)} %collective-permute-done.6.rest_6_), channel_id=1, source_target_pairs={{8,0},{0,8},{24,16},{16,24},{40,32},{32,40},{56,48},{48,56},{72,64... | collective-permute-start | bytes 1622024 | tf_op jit(solution)/shard_map/ppermute | solution.py:283
  38.6 8.5 %collective-permute-start.10 = (f32[1,264,256]{2,1,0:T(8,128)S(1)}, f32[1,264,256]{2,1,0:T(8,128)S(1)}, u32[]{:S(2)}, u32[]{:S(2)}) collective-permute-start(f32[1,264,256]{2,1,0:T(8,128)S(1)} %slice.6), channel_id=1, source_target_pairs={{32,0},{40,8},{48,16},{56,24},{64,32},{72,40},{80,48},{88,56},{96,... | collective-permute-start | bytes 811016 | tf_op jit(solution)/shard_map/ppermute | solution.py:283
  40.3 9.4 %collective-permute-start.11 = (f32[1,264,256]{2,1,0:T(8,128)S(1)}, f32[1,264,256]{2,1,0:T(8,128)S(1)}, u32[]{:S(2)}, u32[]{:S(2)}) collective-permute-start(f32[1,264,256]{2,1,0:T(8,128)S(1)} %slice.7), channel_id=1, source_target_pairs={{96,0},{104,8},{112,16},{120,24},{0,32},{8,40},{16,48},{24,56},{32... | collective-permute-start | bytes 811016 | tf_op jit(solution)/shard_map/ppermute | solution.py:283
  40.6 9.6 %collective-permute-start.12 = (f32[2,264,256]{2,1,0:T(8,128)S(1)}, f32[2,264,256]{2,1,0:T(8,128)S(1)}, u32[]{:S(2)}, u32[]{:S(2)}) collective-permute-start(f32[2,264,256]{2,1,0:T(8,128)S(1)} %collective-permute-done.4.rest_4_), channel_id=1, source_target_pairs={{8,0},{0,8},{24,16},{16,24},{40,32},{32,40},{56,48},{48,56},{72,64... | collective-permute-start | bytes 1622024 | tf_op jit(solution)/shard_map/ppermute | solution.py:283
  44.6 0.9 %copy-start.3 = (f32[1536,128]{1,0:T(8,128)}, f32[1536,128]{1,0:T(8,128)S(1)}, u32[]{:S(2)}) copy-start(f32[1536,128]{1,0:T(8,128)S(1)} %get-tuple-element.41.rest_3_) | copy-start | bytes 2359300
  49.7 1.5 %collective-permute-start.15 = (f32[1,264,256]{2,1,0:T(8,128)S(1)}, f32[1,264,256]{2,1,0:T(8,128)S(1)}, u32[]{:S(2)}, u32[]{:S(2)}) collective-permute-start(f32[1,264,256]{2,1,0:T(8,128)S(1)} %collective-permute-done.10.rest_7_), channel_id=1, source_target_pairs={{8,0},{0,8},{24,16},{16,24},{40,32},{32,40},{56,48},{48,56},{72,64... | collective-permute-start | bytes 811016 | tf_op jit(solution)/shard_map/ppermute | solution.py:283
  49.7 1.9 %collective-permute-start.16 = (f32[1,264,256]{2,1,0:T(8,128)S(1)}, f32[1,264,256]{2,1,0:T(8,128)S(1)}, u32[]{:S(2)}, u32[]{:S(2)}) collective-permute-start(f32[1,264,256]{2,1,0:T(8,128)S(1)} %collective-permute-done.11.rest_8_), channel_id=1, source_target_pairs={{8,0},{0,8},{24,16},{16,24},{40,32},{32,40},{56,48},{48,56},{72,64... | collective-permute-start | bytes 811016 | tf_op jit(solution)/shard_map/ppermute | solution.py:283

commit v3 on v2

--- a/solution.py
+++ b/solution.py
@@ -194,7 +194,7 @@
 
 def cost(rows, n, width):
     return pl.CostEstimate(
-        flops=8 * rows * n * UNIT * width, bytes_accessed=rows * n * UNIT * 4, transcendentals=rows * n * UNIT
+        flops=rows * width, bytes_accessed=rows * width, transcendentals=rows
     )
 
 

time: 85.9 us -> 84.4 us (0.983)
  waiting for transfers between devices: 19.8 us -> 16.6 us
  local copies, waits for them, and re-layouts: 2.5 us -> 4.36 us
    ppermute x17, waiting for transfers between devices: 19.8 us -> 16.6 us  [fetch(): return lax.ppermute(array, 'blk', pairs)]
    unnamed x8 -> x12, local copies, waits for them, and re-layouts: 2.29 us -> 4.15 us
where the time goes in v3:
time: 84.4 us; the launch traced here: 83.2 us
  Pallas kernels  28.7 us (34%)
  blocking collectives  18.8 us (22%)
  waiting for transfers between devices  16.6 us (20%)
  starting transfers between devices  12.6 us (15%)
  local copies, waits for them, and re-layouts  4.36 us (5%)
  other arithmetic  1.95 us (2%)
    all_to_all x1, blocking collectives, body(): lax.all_to_all(sums.reshape(-1, 1, 2 * UNIT), ('blk', 'rows'), 0, 0, tile...  18.8 us
    ppermute x17, waiting for transfers between devices, fetch(): return lax.ppermute(array, 'blk', pairs)  16.6 us
    pallas_call x1, Pallas kernels, closing(): pl.pallas_call(functools.partial(closing_kernel, len(blocks), len(kept),...  13.4 us
    ppermute x17, starting transfers between devices, fetch(): return lax.ppermute(array, 'blk', pairs)  12.6 us
    pallas_call x2, Pallas kernels, middle(): pl.pallas_call(functools.partial(middle_kernel, len(blocks), group), in_s...  12.2 us
    unnamed x12, local copies, waits for them, and re-layouts  4.15 us
    pallas_call x1, Pallas kernels, opening(): pl.pallas_call(functools.partial(opening_kernel, group), in_specs=[VMEM]...  3.14 us
  transfers between devices with their start and end apart: 17, of which 8 were waited for; matrix products, arithmetic and copies ran while one was open for 0% of the time, Pallas kernels for 18%

profile of v3, /device:TPU:0, one launch (start us, length us, event | category | flops | bytes accessed | tf_op | source)
XLA Modules:
  0.0 83.2 jit_solution(6012826174692678118)
XLA Ops:
  0.1 1.2 %maximum_maximum_fusion.rest_0_ = f32[2,264,256]{2,1,0:T(8,128)S(1)} fusion(f32[2,1,256]{2,1,0:T(1,128)} %bitcast.21, f32[2,256,256]{2,1,0:T(8,128)} %bitcast.20, f32[264]{0:T(512)S(1)} %pad.2.clone), kind=kLoop, calls=%fused_computation | loop fusion | flops 270336 | bytes 1068064 | tf_op jit(solution)/shard_map/concatenate | solution.py:291
  1.3 2.9 %collective-permute-start = (f32[2,264,256]{2,1,0:T(8,128)S(1)}, f32[2,264,256]{2,1,0:T(8,128)S(1)}, u32[]{:S(2)}, u32[]{:S(2)}) collective-permute-start(f32[2,264,256]{2,1,0:T(8,128)S(1)} %maximum_maximum_fusion.rest_0_), channel_id=1, source_target_pairs={{32,0},{40,8},{48,16},{56,24},{64,32},{72,40},{80,48},{88,56},{96,... | collective-permute-start | bytes 1622024 | tf_op jit(solution)/shard_map/ppermute | solution.py:283
  4.3 1.9 %collective-permute-start.2 = (f32[2,264,256]{2,1,0:T(8,128)S(1)}, f32[2,264,256]{2,1,0:T(8,128)S(1)}, u32[]{:S(2)}, u32[]{:S(2)}) collective-permute-start(f32[2,264,256]{2,1,0:T(8,128)S(1)} %maximum_maximum_fusion.rest_0_), channel_id=1, source_target_pairs={{16,0},{24,8},{0,16},{8,24},{48,32},{56,40},{32,48},{40,56},{80,64... | collective-permute-start | bytes 1622024 | tf_op jit(solution)/shard_map/ppermute | solution.py:283
  6.3 0.8 copy-done.4
  7.1 1.4 %copy-done.2 = f32[1536,256]{1,0:T(8,128)S(1)} copy-done((f32[1536,256]{1,0:T(8,128)S(1)}, f32[1536,256]{1,0:T(8,128)}, u32[]{:S(2)}) %copy-start.2) | copy-done | bytes 1572888
  8.5 1.0 %copy-done.5 = f32[2,264,256]{2,1,0:T(8,128)S(1)} copy-done((f32[2,264,256]{2,1,0:T(8,128)S(1)}, f32[2,264,256]{2,1,0:T(8,128)}, u32[]{:S(2)}) %copy-start.5) | copy-done | bytes 540696
  9.5 3.1 %opening.1 = (bf16[1536,256]{1,0:T(8,128)(2,1)S(1)}, f8e4m3fn[1536,512]{1,0:T(32,128)(4,1)S(1)}, f32[1536,128]{1,0:T(8,128)S(1)}, f32[1536,128]{1,0:T(8,128)S(1)}, f32[4,1536,256]{2,1,0:T(8,128)S(1)}) custom-call(f32[1536,256]{1,0:T(8,128)S(1)} %copy-done.2, f32[2,264,256]{2,1,0:T(8,128)S(1)} %maximum_maximum_fusion.rest_0_, f32[2,264,256]{2,1,0:T(8,128)S(1)} %copy-done.5), custom_call_target="tpu_custom_call" | custom-call | flops 393216 | bytes 393216 | tf_op jit(solution)/shard_map/opening/pallas_call | solution.py:212
  12.7 3.7 %collective-permute-done.rest_4_ = f32[2,264,256]{2,1,0:T(8,128)S(1)} collective-permute-done((f32[2,264,256]{2,1,0:T(8,128)S(1)}, f32[2,264,256]{2,1,0:T(8,128)S(1)}, u32[]{:S(2)}, u32[]{:S(2)}) %collective-permute-start) | collective-permute-done | bytes 540704 | tf_op jit(solution)/shard_map/ppermute | solution.py:283
  16.4 3.4 %collective-permute-done.1.rest_5_ = f32[2,264,256]{2,1,0:T(8,128)S(1)} collective-permute-done((f32[2,264,256]{2,1,0:T(8,128)S(1)}, f32[2,264,256]{2,1,0:T(8,128)S(1)}, u32[]{:S(2)}, u32[]{:S(2)}) %collective-permute-start.1) | collective-permute-done | bytes 540704 | tf_op jit(solution)/shard_map/ppermute | solution.py:283
  19.8 0.5 collective-permute-start.8
  20.3 1.9 %collective-permute-start.4 = (f32[2,264,256]{2,1,0:T(8,128)S(1)}, f32[2,264,256]{2,1,0:T(8,128)S(1)}, u32[]{:S(2)}, u32[]{:S(2)}) collective-permute-start(f32[2,264,256]{2,1,0:T(8,128)S(1)} %collective-permute-done.rest_4_), channel_id=1, source_target_pairs={{32,0},{40,8},{48,16},{56,24},{64,32},{72,40},{80,48},{88,56},{96,... | collective-permute-start | bytes 1622024 | tf_op jit(solution)/shard_map/ppermute | solution.py:283
  22.4 1.9 %collective-permute-start.6 = (f32[2,264,256]{2,1,0:T(8,128)S(1)}, f32[2,264,256]{2,1,0:T(8,128)S(1)}, u32[]{:S(2)}, u32[]{:S(2)}) collective-permute-start(f32[2,264,256]{2,1,0:T(8,128)S(1)} %collective-permute-done.rest_4_), channel_id=1, source_target_pairs={{16,0},{24,8},{0,16},{8,24},{48,32},{56,40},{32,48},{40,56},{80,64... | collective-permute-start | bytes 1622024 | tf_op jit(solution)/shard_map/ppermute | solution.py:283
  24.3 8.3 %middle.2 = (f32[1536,128]{1,0:T(8,128)S(1)}, f32[12,1536,256]{2,1,0:T(8,128)}) custom-call(bf16[1536,256]{1,0:T(8,128)(2,1)S(1)} %get-tuple-element.28.rest_0_, f8e4m3fn[1536,512]{1,0:T(32,128)(4,1)S(1)} %get-tuple-element.29.rest_1_, f32[1536,128]{1,0:T(8,128)S(1)} %get-tuple-element.30.rest_2_, f32[1536,128]{1,0:T(8,128)S(1)} %get-tuple-element.33.rest_3_, ...), custom_call_target="tpu_custom_call" | custom-call | flops 393216 | bytes 393216 | tf_op jit(solution)/shard_map/middle/pallas_call | solution.py:227
  32.6 2.4 %collective-permute-done.4.rest_4_ = f32[2,264,256]{2,1,0:T(8,128)S(1)} collective-permute-done((f32[2,264,256]{2,1,0:T(8,128)S(1)}, f32[2,264,256]{2,1,0:T(8,128)S(1)}, u32[]{:S(2)}, u32[]{:S(2)}) %collective-permute-start.4) | collective-permute-done | bytes 540704 | tf_op jit(solution)/shard_map/ppermute | solution.py:283
  35.0 2.8 %collective-permute-done.5.rest_5_ = f32[2,264,256]{2,1,0:T(8,128)S(1)} collective-permute-done((f32[2,264,256]{2,1,0:T(8,128)S(1)}, f32[2,264,256]{2,1,0:T(8,128)S(1)}, u32[]{:S(2)}, u32[]{:S(2)}) %collective-permute-start.5) | collective-permute-done | bytes 540704 | tf_op jit(solution)/shard_map/ppermute | solution.py:283
  37.9 1.8 %collective-permute-start.10 = (f32[1,264,256]{2,1,0:T(8,128)S(1)}, f32[1,264,256]{2,1,0:T(8,128)S(1)}, u32[]{:S(2)}, u32[]{:S(2)}) collective-permute-start(f32[1,264,256]{2,1,0:T(8,128)S(1)} %slice.6), channel_id=1, source_target_pairs={{32,0},{40,8},{48,16},{56,24},{64,32},{72,40},{80,48},{88,56},{96,... | collective-permute-start | bytes 811016 | tf_op jit(solution)/shard_map/ppermute | solution.py:283
  40.6 3.9 %middle.3 = (f32[1536,128]{1,0:T(8,128)S(1)}, f32[6,1536,256]{2,1,0:T(8,128)S(1)}) custom-call(bf16[1536,256]{1,0:T(8,128)(2,1)S(1)} %get-tuple-element.28.rest_0_, f8e4m3fn[1536,512]{1,0:T(32,128)(4,1)S(1)} %get-tuple-element.29.rest_1_, f32[1536,128]{1,0:T(8,128)S(1)} %get-tuple-element.30.rest_2_, f32[1536,128]{1,0:T(8,128)S(1)} %get-tuple-element.38.rest_3_, ...), custom_call_target="tpu_custom_call" | custom-call | flops 393216 | bytes 393216 | tf_op jit(solution)/shard_map/middle/pallas_call | solution.py:227
  44.5 0.9 %copy-done.3 = f32[1536,128]{1,0:T(8,128)} copy-done((f32[1536,128]{1,0:T(8,128)}, f32[1536,128]{1,0:T(8,128)S(1)}, u32[]{:S(2)}) %copy-start.3) | copy-done | bytes 786456
  45.7 2.4 %collective-permute-done.11.rest_8_ = f32[1,264,256]{2,1,0:T(8,128)S(1)} collective-permute-done((f32[1,264,256]{2,1,0:T(8,128)S(1)}, f32[1,264,256]{2,1,0:T(8,128)S(1)}, u32[]{:S(2)}, u32[]{:S(2)}) %collective-permute-start.11) | collective-permute-done | bytes 270368 | tf_op jit(solution)/shard_map/ppermute | solution.py:283
  48.2 0.5 collective-permute-start.16
  48.7 1.0 %collective-permute-done.15.rest_9_ = f32[1,264,256]{2,1,0:T(8,128)S(1)} collective-permute-done((f32[1,264,256]{2,1,0:T(8,128)S(1)}, f32[1,264,256]{2,1,0:T(8,128)S(1)}, u32[]{:S(2)}, u32[]{:S(2)}) %collective-permute-start.15) | collective-permute-done | bytes 270368 | tf_op jit(solution)/shard_map/ppermute | solution.py:283
  50.1 13.4 %closing.1 = f32[16,8,1,512]{3,2,1,0:T(1,128)S(1)} custom-call(s32[16]{0:T(128)S(1)} %stack.67.place_ref, bf16[1536,256]{1,0:T(8,128)(2,1)S(1)} %get-tuple-element.28.rest_0_, f8e4m3fn[1536,512]{1,0:T(32,128)(4,1)} %copy-done, f32[1536,128]{1,0:T(8,128)} %copy-done.1, f32[1536,128]{1,0:T(8,128)} %copy-done.3, ...), custom_call_target="tpu_custom_call" | custom-call | flops 393216 | bytes 393216 | tf_op jit(solution)/shard_map/closing/pallas_call | solution.py:248
  63.5 18.8 %all_to_all.5 = f32[128,1,512]{2,1,0:T(1,128)S(1)} all-to-all(f32[128,1,512]{2,1,0:T(1,128)S(1)} %bitcast.19), channel_id=1, replica_groups=mesh['blk'=16,'rows'=8] {'blk','rows'}, dimensions={0} | all-to-all | bytes 524288 | tf_op jit(solution)/shard_map/all_to_all | solution.py:329
  82.6 0.6 broadcast_multiply_fusion
  (35 shorter events, 2.3 us)
Async XLA Ops:
  1.2 5.0 %collective-permute-start.3 = (f32[2,264,256]{2,1,0:T(8,128)S(1)}, f32[2,264,256]{2,1,0:T(8,128)S(1)}, u32[]{:S(2)}, u32[]{:S(2)}) collective-permute-start(f32[2,264,256]{2,1,0:T(8,128)S(1)} %maximum_maximum_fusion.rest_0_), channel_id=1, source_target_pairs={{8,0},{0,8},{24,16},{16,24},{40,32},{32,40},{56,48},{48,56},{72,64... | collective-permute-start | bytes 1622024 | tf_op jit(solution)/shard_map/ppermute | solution.py:283
  1.3 15.1 %collective-permute-start = (f32[2,264,256]{2,1,0:T(8,128)S(1)}, f32[2,264,256]{2,1,0:T(8,128)S(1)}, u32[]{:S(2)}, u32[]{:S(2)}) collective-permute-start(f32[2,264,256]{2,1,0:T(8,128)S(1)} %maximum_maximum_fusion.rest_0_), channel_id=1, source_target_pairs={{32,0},{40,8},{48,16},{56,24},{64,32},{72,40},{80,48},{88,56},{96,... | collective-permute-start | bytes 1622024 | tf_op jit(solution)/shard_map/ppermute | solution.py:283
  4.2 15.6 %collective-permute-start.1 = (f32[2,264,256]{2,1,0:T(8,128)S(1)}, f32[2,264,256]{2,1,0:T(8,128)S(1)}, u32[]{:S(2)}, u32[]{:S(2)}) collective-permute-start(f32[2,264,256]{2,1,0:T(8,128)S(1)} %maximum_maximum_fusion.rest_0_), channel_id=1, source_target_pairs={{96,0},{104,8},{112,16},{120,24},{0,32},{8,40},{16,48},{24,56},{32... | collective-permute-start | bytes 1622024 | tf_op jit(solution)/shard_map/ppermute | solution.py:283
  4.3 15.6 %collective-permute-start.2 = (f32[2,264,256]{2,1,0:T(8,128)S(1)}, f32[2,264,256]{2,1,0:T(8,128)S(1)}, u32[]{:S(2)}, u32[]{:S(2)}) collective-permute-start(f32[2,264,256]{2,1,0:T(8,128)S(1)} %maximum_maximum_fusion.rest_0_), channel_id=1, source_target_pairs={{16,0},{24,8},{0,16},{8,24},{48,32},{56,40},{32,48},{40,56},{80,64... | collective-permute-start | bytes 1622024 | tf_op jit(solution)/shard_map/ppermute | solution.py:283
  6.3 0.8 copy-start.4
  7.1 1.4 %copy-start.2 = (f32[1536,256]{1,0:T(8,128)S(1)}, f32[1536,256]{1,0:T(8,128)}, u32[]{:S(2)}) copy-start(f32[1536,256]{1,0:T(8,128)} %x_ref.1) | copy-start | bytes 4718596
  8.5 1.0 %copy-start.5 = (f32[2,264,256]{2,1,0:T(8,128)S(1)}, f32[2,264,256]{2,1,0:T(8,128)}, u32[]{:S(2)}) copy-start(f32[2,264,256]{2,1,0:T(8,128)} %copy-done.4) | copy-start | bytes 1622020
  12.7 37.4 %copy-start = (f8e4m3fn[1536,512]{1,0:T(32,128)(4,1)}, f8e4m3fn[1536,512]{1,0:T(32,128)(4,1)S(1)}, u32[]{:S(2)}) copy-start(f8e4m3fn[1536,512]{1,0:T(32,128)(4,1)S(1)} %get-tuple-element.29.rest_1_) | copy-start | bytes 2359300
  12.7 37.4 %copy-start.1 = (f32[1536,128]{1,0:T(8,128)}, f32[1536,128]{1,0:T(8,128)S(1)}, u32[]{:S(2)}) copy-start(f32[1536,128]{1,0:T(8,128)S(1)} %get-tuple-element.30.rest_2_) | copy-start | bytes 2359300
  19.8 2.5 %collective-permute-start.7 = (f32[2,264,256]{2,1,0:T(8,128)S(1)}, f32[2,264,256]{2,1,0:T(8,128)S(1)}, u32[]{:S(2)}, u32[]{:S(2)}) collective-permute-start(f32[2,264,256]{2,1,0:T(8,128)S(1)} %collective-permute-done.rest_4_), channel_id=1, source_target_pairs={{8,0},{0,8},{24,16},{16,24},{40,32},{32,40},{56,48},{48,56},{72,64... | collective-permute-start | bytes 1622024 | tf_op jit(solution)/shard_map/ppermute | solution.py:283
  19.8 4.5 %collective-permute-start.8 = (f32[2,264,256]{2,1,0:T(8,128)S(1)}, f32[2,264,256]{2,1,0:T(8,128)S(1)}, u32[]{:S(2)}, u32[]{:S(2)}) collective-permute-start(f32[2,264,256]{2,1,0:T(8,128)S(1)} %collective-permute-done.1.rest_5_), channel_id=1, source_target_pairs={{8,0},{0,8},{24,16},{16,24},{40,32},{32,40},{56,48},{48,56},{72,64... | collective-permute-start | bytes 1622024 | tf_op jit(solution)/shard_map/ppermute | solution.py:283
  20.3 4.0 %collective-permute-start.9 = (f32[2,264,256]{2,1,0:T(8,128)S(1)}, f32[2,264,256]{2,1,0:T(8,128)S(1)}, u32[]{:S(2)}, u32[]{:S(2)}) collective-permute-start(f32[2,264,256]{2,1,0:T(8,128)S(1)} %collective-permute-done.2.rest_6_), channel_id=1, source_target_pairs={{8,0},{0,8},{24,16},{16,24},{40,32},{32,40},{56,48},{48,56},{72,64... | collective-permute-start | bytes 1622024 | tf_op jit(solution)/shard_map/ppermute | solution.py:283
  20.3 14.7 %collective-permute-start.4 = (f32[2,264,256]{2,1,0:T(8,128)S(1)}, f32[2,264,256]{2,1,0:T(8,128)S(1)}, u32[]{:S(2)}, u32[]{:S(2)}) collective-permute-start(f32[2,264,256]{2,1,0:T(8,128)S(1)} %collective-permute-done.rest_4_), channel_id=1, source_target_pairs={{32,0},{40,8},{48,16},{56,24},{64,32},{72,40},{80,48},{88,56},{96,... | collective-permute-start | bytes 1622024 | tf_op jit(solution)/shard_map/ppermute | solution.py:283
  22.2 15.6 %collective-permute-start.5 = (f32[2,264,256]{2,1,0:T(8,128)S(1)}, f32[2,264,256]{2,1,0:T(8,128)S(1)}, u32[]{:S(2)}, u32[]{:S(2)}) collective-permute-start(f32[2,264,256]{2,1,0:T(8,128)S(1)} %collective-permute-done.2.rest_6_), channel_id=1, source_target_pairs={{96,0},{104,8},{112,16},{120,24},{0,32},{8,40},{16,48},{24,56},{32... | collective-permute-start | bytes 1622024 | tf_op jit(solution)/shard_map/ppermute | solution.py:283
  22.4 15.5 %collective-permute-start.6 = (f32[2,264,256]{2,1,0:T(8,128)S(1)}, f32[2,264,256]{2,1,0:T(8,128)S(1)}, u32[]{:S(2)}, u32[]{:S(2)}) collective-permute-start(f32[2,264,256]{2,1,0:T(8,128)S(1)} %collective-permute-done.rest_4_), channel_id=1, source_target_pairs={{16,0},{24,8},{0,16},{8,24},{48,32},{56,40},{32,48},{40,56},{80,64... | collective-permute-start | bytes 1622024 | tf_op jit(solution)/shard_map/ppermute | solution.py:283
  37.9 7.9 %collective-permute-start.10 = (f32[1,264,256]{2,1,0:T(8,128)S(1)}, f32[1,264,256]{2,1,0:T(8,128)S(1)}, u32[]{:S(2)}, u32[]{:S(2)}) collective-permute-start(f32[1,264,256]{2,1,0:T(8,128)S(1)} %slice.6), channel_id=1, source_target_pairs={{32,0},{40,8},{48,16},{56,24},{64,32},{72,40},{80,48},{88,56},{96,... | collective-permute-start | bytes 811016 | tf_op jit(solution)/shard_map/ppermute | solution.py:283
  39.7 8.5 %collective-permute-start.11 = (f32[1,264,256]{2,1,0:T(8,128)S(1)}, f32[1,264,256]{2,1,0:T(8,128)S(1)}, u32[]{:S(2)}, u32[]{:S(2)}) collective-permute-start(f32[1,264,256]{2,1,0:T(8,128)S(1)} %slice.7), channel_id=1, source_target_pairs={{96,0},{104,8},{112,16},{120,24},{0,32},{8,40},{16,48},{24,56},{32... | collective-permute-start | bytes 811016 | tf_op jit(solution)/shard_map/ppermute | solution.py:283
  40.1 8.6 %collective-permute-start.12 = (f32[2,264,256]{2,1,0:T(8,128)S(1)}, f32[2,264,256]{2,1,0:T(8,128)S(1)}, u32[]{:S(2)}, u32[]{:S(2)}) collective-permute-start(f32[2,264,256]{2,1,0:T(8,128)S(1)} %collective-permute-done.4.rest_4_), channel_id=1, source_target_pairs={{8,0},{0,8},{24,16},{16,24},{40,32},{32,40},{56,48},{48,56},{72,64... | collective-permute-start | bytes 1622024 | tf_op jit(solution)/shard_map/ppermute | solution.py:283
  40.1 8.6 %collective-permute-start.13 = (f32[2,264,256]{2,1,0:T(8,128)S(1)}, f32[2,264,256]{2,1,0:T(8,128)S(1)}, u32[]{:S(2)}, u32[]{:S(2)}) collective-permute-start(f32[2,264,256]{2,1,0:T(8,128)S(1)} %collective-permute-done.5.rest_5_), channel_id=1, source_target_pairs={{8,0},{0,8},{24,16},{16,24},{40,32},{32,40},{56,48},{48,56},{72,64... | collective-permute-start | bytes 1622024 | tf_op jit(solution)/shard_map/ppermute | solution.py:283
  40.6 8.1 %collective-permute-start.14 = (f32[2,264,256]{2,1,0:T(8,128)S(1)}, f32[2,264,256]{2,1,0:T(8,128)S(1)}, u32[]{:S(2)}, u32[]{:S(2)}) collective-permute-start(f32[2,264,256]{2,1,0:T(8,128)S(1)} %collective-permute-done.6.rest_6_), channel_id=1, source_target_pairs={{8,0},{0,8},{24,16},{16,24},{40,32},{32,40},{56,48},{48,56},{72,64... | collective-permute-start | bytes 1622024 | tf_op jit(solution)/shard_map/ppermute | solution.py:283
  44.5 0.9 %copy-start.3 = (f32[1536,128]{1,0:T(8,128)}, f32[1536,128]{1,0:T(8,128)S(1)}, u32[]{:S(2)}) copy-start(f32[1536,128]{1,0:T(8,128)S(1)} %get-tuple-element.41.rest_3_) | copy-start | bytes 2359300
  48.2 1.5 %collective-permute-start.15 = (f32[1,264,256]{2,1,0:T(8,128)S(1)}, f32[1,264,256]{2,1,0:T(8,128)S(1)}, u32[]{:S(2)}, u32[]{:S(2)}) collective-permute-start(f32[1,264,256]{2,1,0:T(8,128)S(1)} %collective-permute-done.10.rest_7_), channel_id=1, source_target_pairs={{8,0},{0,8},{24,16},{16,24},{40,32},{32,40},{56,48},{48,56},{72,64... | collective-permute-start | bytes 811016 | tf_op jit(solution)/shard_map/ppermute | solution.py:283
  48.2 1.9 %collective-permute-start.16 = (f32[1,264,256]{2,1,0:T(8,128)S(1)}, f32[1,264,256]{2,1,0:T(8,128)S(1)}, u32[]{:S(2)}, u32[]{:S(2)}) collective-permute-start(f32[1,264,256]{2,1,0:T(8,128)S(1)} %collective-permute-done.11.rest_8_), channel_id=1, source_target_pairs={{8,0},{0,8},{24,16},{16,24},{40,32},{32,40},{56,48},{48,56},{72,64... | collective-permute-start | bytes 811016 | tf_op jit(solution)/shard_map/ppermute | solution.py:283

commit v4 on v3

--- a/solution.py
+++ b/solution.py
@@ -126,9 +126,9 @@
 
 
 def closing_kernel(n, m, f, group, place_ref, *rest):
-    sources, units, kept, saved = rest[:4], rest[4 : 4 + n], rest[4 + n : 4 + n + m], rest[4 + n + m : 4 + n + m + f]
-    out, xh, x8, a, v_in, v, sums, k, *prepared, held, points_sem, sem = rest[4 + n + m + f :]
-    copies = load(sources, (xh, x8, a, v_in), points_sem)
+    sources, v_in, units, kept, saved = rest[:3], rest[3], rest[4 : 4 + n], rest[4 + n : 4 + n + m], rest[4 + n + m : 4 + n + m + f]
+    out, xh, x8, a, v, sums, k, *prepared, held, points_sem, sem = rest[4 + n + m + f :]
+    copies = load(sources, (xh, x8, a), points_sem)
     (saved,) = saved
     early = held.shape[0]
     late = saved.shape[0] - early
@@ -228,7 +228,7 @@
         functools.partial(middle_kernel, len(blocks), group),
         in_specs=[ANY] * 4 + [VMEM] * len(blocks),
         out_specs=[VMEM, VMEM if keep else HBM],
-        out_shape=[of((rows, 128)), (pltpu.VMEM((n, rows, UNIT), F32) if keep else of((n, rows, UNIT)))],
+        out_shape=[pltpu.VMEM((rows, 128), F32) if keep else of((rows, 128)), (pltpu.VMEM((n, rows, UNIT), F32) if keep else of((n, rows, UNIT)))],
         scratch_shapes=[
             *points_scratch(rows, width),
             *prepared_scratch(n, width),
@@ -247,23 +247,23 @@
     total = n + count(kept) + count(saved)
     return pl.pallas_call(
         functools.partial(closing_kernel, len(blocks), len(kept), len(saved), group),
-        in_specs=[pl.BlockSpec(memory_space=pltpu.SMEM)] + [ANY] * 4 + [VMEM] * (len(blocks) + len(kept)) + [HBM] * len(saved),
+        in_specs=[pl.BlockSpec(memory_space=pltpu.SMEM)] + [ANY] * 3 + [VMEM] * (1 + len(blocks) + len(kept)) + [HBM] * len(saved),
         out_specs=VMEM,
         out_shape=of((total // 2, copies, 1, 2 * UNIT)),
         scratch_shapes=[
-            *points_scratch(rows, width),
+            *points_scratch(rows, width)[:3],
             pltpu.VMEM((rows, 128), F32),
             pltpu.VMEM((total, 1, UNIT), F32),
             pltpu.VMEM((n, rows, UNIT), F32),
             *prepared_scratch(n, width),
             pltpu.VMEM((early, rows, UNIT), F32),
-            pltpu.SemaphoreType.DMA((4,)),
+            pltpu.SemaphoreType.DMA((3,)),
             pltpu.SemaphoreType.DMA((2,)),
         ],
         cost_estimate=cost(rows, 2 * n, width),
         compiler_params=pltpu.CompilerParams(vmem_limit_bytes=GRANT),
         name="closing",
-    )(place, xh, x8, a, v, *blocks, *[pltpu.with_memory_space_constraint(k, pltpu.VMEM) for k in kept], *saved)
+    )(place, xh, x8, a, pltpu.with_memory_space_constraint(v, pltpu.VMEM), *blocks, *[pltpu.with_memory_space_constraint(k, pltpu.VMEM) for k in kept], *saved)
 
 
 RING, PAIR, CORES = 4, 2, 2

time: 84.4 us -> 84.4 us (level)
  waiting for transfers between devices: 16.6 us -> 17.5 us
  local copies, waits for them, and re-layouts: 4.36 us -> 3.48 us
    ppermute x17, waiting for transfers between devices: 16.6 us -> 17.5 us  [fetch(): return lax.ppermute(array, 'blk', pairs)]
    unnamed x12, local copies, waits for them, and re-layouts: 4.15 us -> 3.27 us
where the time goes in v4:
time: 84.4 us; the launch traced here: 83.1 us
  Pallas kernels  28.7 us (34%)
  blocking collectives  18.8 us (22%)
  waiting for transfers between devices  17.5 us (21%)
  starting transfers between devices  12.6 us (15%)
  local copies, waits for them, and re-layouts  3.48 us (4%)
  other arithmetic  1.95 us (2%)
    all_to_all x1, blocking collectives, body(): lax.all_to_all(sums.reshape(-1, 1, 2 * UNIT), ('blk', 'rows'), 0, 0, tile...  18.8 us
    ppermute x17, waiting for transfers between devices, fetch(): return lax.ppermute(array, 'blk', pairs)  17.5 us
    pallas_call x1, Pallas kernels, closing(): pl.pallas_call(functools.partial(closing_kernel, len(blocks), len(kept),...  13.3 us
    ppermute x17, starting transfers between devices, fetch(): return lax.ppermute(array, 'blk', pairs)  12.6 us
    pallas_call x2, Pallas kernels, middle(): pl.pallas_call(functools.partial(middle_kernel, len(blocks), group), in_s...  12.2 us
    unnamed x12, local copies, waits for them, and re-layouts  3.27 us
    pallas_call x1, Pallas kernels, opening(): pl.pallas_call(functools.partial(opening_kernel, group), in_specs=[VMEM]...  3.14 us
  transfers between devices with their start and end apart: 17, of which 8 were waited for; matrix products, arithmetic and copies ran while one was open for 0% of the time, Pallas kernels for 18%

profile of v4, /device:TPU:0, one launch (start us, length us, event | category | flops | bytes accessed | tf_op | source)
XLA Modules:
  0.0 83.1 jit_solution(6311783284474429138)
XLA Ops:
  0.1 1.2 %maximum_maximum_fusion.rest_0_ = f32[2,264,256]{2,1,0:T(8,128)S(1)} fusion(f32[2,1,256]{2,1,0:T(1,128)} %bitcast.21, f32[2,256,256]{2,1,0:T(8,128)} %bitcast.20, f32[264]{0:T(512)S(1)} %pad.2.clone), kind=kLoop, calls=%fused_computation | loop fusion | flops 270336 | bytes 1068064 | tf_op jit(solution)/shard_map/concatenate | solution.py:291
  1.3 2.9 %collective-permute-start = (f32[2,264,256]{2,1,0:T(8,128)S(1)}, f32[2,264,256]{2,1,0:T(8,128)S(1)}, u32[]{:S(2)}, u32[]{:S(2)}) collective-permute-start(f32[2,264,256]{2,1,0:T(8,128)S(1)} %maximum_maximum_fusion.rest_0_), channel_id=1, source_target_pairs={{32,0},{40,8},{48,16},{56,24},{64,32},{72,40},{80,48},{88,56},{96,... | collective-permute-start | bytes 1622024 | tf_op jit(solution)/shard_map/ppermute | solution.py:283
  4.3 1.9 %collective-permute-start.2 = (f32[2,264,256]{2,1,0:T(8,128)S(1)}, f32[2,264,256]{2,1,0:T(8,128)S(1)}, u32[]{:S(2)}, u32[]{:S(2)}) collective-permute-start(f32[2,264,256]{2,1,0:T(8,128)S(1)} %maximum_maximum_fusion.rest_0_), channel_id=1, source_target_pairs={{16,0},{24,8},{0,16},{8,24},{48,32},{56,40},{32,48},{40,56},{80,64... | collective-permute-start | bytes 1622024 | tf_op jit(solution)/shard_map/ppermute | solution.py:283
  6.3 0.8 copy-done.4
  7.1 1.4 %copy-done.3 = f32[1536,256]{1,0:T(8,128)S(1)} copy-done((f32[1536,256]{1,0:T(8,128)S(1)}, f32[1536,256]{1,0:T(8,128)}, u32[]{:S(2)}) %copy-start.3) | copy-done | bytes 1572888
  8.5 1.0 %copy-done.5 = f32[2,264,256]{2,1,0:T(8,128)S(1)} copy-done((f32[2,264,256]{2,1,0:T(8,128)S(1)}, f32[2,264,256]{2,1,0:T(8,128)}, u32[]{:S(2)}) %copy-start.5) | copy-done | bytes 540696
  9.5 3.1 %opening.1 = (bf16[1536,256]{1,0:T(8,128)(2,1)S(1)}, f8e4m3fn[1536,512]{1,0:T(32,128)(4,1)S(1)}, f32[1536,128]{1,0:T(8,128)S(1)}, f32[1536,128]{1,0:T(8,128)S(1)}, f32[4,1536,256]{2,1,0:T(8,128)S(1)}) custom-call(f32[1536,256]{1,0:T(8,128)S(1)} %copy-done.3, f32[2,264,256]{2,1,0:T(8,128)S(1)} %maximum_maximum_fusion.rest_0_, f32[2,264,256]{2,1,0:T(8,128)S(1)} %copy-done.5), custom_call_target="tpu_custom_call" | custom-call | flops 393216 | bytes 393216 | tf_op jit(solution)/shard_map/opening/pallas_call | solution.py:212
  12.7 3.7 %collective-permute-done.rest_4_ = f32[2,264,256]{2,1,0:T(8,128)S(1)} collective-permute-done((f32[2,264,256]{2,1,0:T(8,128)S(1)}, f32[2,264,256]{2,1,0:T(8,128)S(1)}, u32[]{:S(2)}, u32[]{:S(2)}) %collective-permute-start) | collective-permute-done | bytes 540704 | tf_op jit(solution)/shard_map/ppermute | solution.py:283
  16.4 3.4 %collective-permute-done.1.rest_5_ = f32[2,264,256]{2,1,0:T(8,128)S(1)} collective-permute-done((f32[2,264,256]{2,1,0:T(8,128)S(1)}, f32[2,264,256]{2,1,0:T(8,128)S(1)}, u32[]{:S(2)}, u32[]{:S(2)}) %collective-permute-start.1) | collective-permute-done | bytes 540704 | tf_op jit(solution)/shard_map/ppermute | solution.py:283
  19.8 0.5 collective-permute-start.8
  20.3 1.9 %collective-permute-start.4 = (f32[2,264,256]{2,1,0:T(8,128)S(1)}, f32[2,264,256]{2,1,0:T(8,128)S(1)}, u32[]{:S(2)}, u32[]{:S(2)}) collective-permute-start(f32[2,264,256]{2,1,0:T(8,128)S(1)} %collective-permute-done.rest_4_), channel_id=1, source_target_pairs={{32,0},{40,8},{48,16},{56,24},{64,32},{72,40},{80,48},{88,56},{96,... | collective-permute-start | bytes 1622024 | tf_op jit(solution)/shard_map/ppermute | solution.py:283
  22.4 1.9 %collective-permute-start.6 = (f32[2,264,256]{2,1,0:T(8,128)S(1)}, f32[2,264,256]{2,1,0:T(8,128)S(1)}, u32[]{:S(2)}, u32[]{:S(2)}) collective-permute-start(f32[2,264,256]{2,1,0:T(8,128)S(1)} %collective-permute-done.rest_4_), channel_id=1, source_target_pairs={{16,0},{24,8},{0,16},{8,24},{48,32},{56,40},{32,48},{40,56},{80,64... | collective-permute-start | bytes 1622024 | tf_op jit(solution)/shard_map/ppermute | solution.py:283
  24.3 8.3 %middle.2 = (f32[1536,128]{1,0:T(8,128)S(1)}, f32[12,1536,256]{2,1,0:T(8,128)}) custom-call(bf16[1536,256]{1,0:T(8,128)(2,1)S(1)} %get-tuple-element.28.rest_0_, f8e4m3fn[1536,512]{1,0:T(32,128)(4,1)S(1)} %get-tuple-element.29.rest_1_, f32[1536,128]{1,0:T(8,128)S(1)} %get-tuple-element.30.rest_2_, f32[1536,128]{1,0:T(8,128)S(1)} %get-tuple-element.33.rest_3_, ...), custom_call_target="tpu_custom_call" | custom-call | flops 393216 | bytes 393216 | tf_op jit(solution)/shard_map/middle/pallas_call | solution.py:227
  32.6 2.4 %collective-permute-done.4.rest_4_ = f32[2,264,256]{2,1,0:T(8,128)S(1)} collective-permute-done((f32[2,264,256]{2,1,0:T(8,128)S(1)}, f32[2,264,256]{2,1,0:T(8,128)S(1)}, u32[]{:S(2)}, u32[]{:S(2)}) %collective-permute-start.4) | collective-permute-done | bytes 540704 | tf_op jit(solution)/shard_map/ppermute | solution.py:283
  35.0 2.8 %collective-permute-done.5.rest_5_ = f32[2,264,256]{2,1,0:T(8,128)S(1)} collective-permute-done((f32[2,264,256]{2,1,0:T(8,128)S(1)}, f32[2,264,256]{2,1,0:T(8,128)S(1)}, u32[]{:S(2)}, u32[]{:S(2)}) %collective-permute-start.5) | collective-permute-done | bytes 540704 | tf_op jit(solution)/shard_map/ppermute | solution.py:283
  37.9 1.8 %collective-permute-start.10 = (f32[1,264,256]{2,1,0:T(8,128)S(1)}, f32[1,264,256]{2,1,0:T(8,128)S(1)}, u32[]{:S(2)}, u32[]{:S(2)}) collective-permute-start(f32[1,264,256]{2,1,0:T(8,128)S(1)} %slice.6), channel_id=1, source_target_pairs={{32,0},{40,8},{48,16},{56,24},{64,32},{72,40},{80,48},{88,56},{96,... | collective-permute-start | bytes 811016 | tf_op jit(solution)/shard_map/ppermute | solution.py:283
  40.6 3.9 %middle.3 = (f32[1536,128]{1,0:T(8,128)S(1)}, f32[6,1536,256]{2,1,0:T(8,128)S(1)}) custom-call(bf16[1536,256]{1,0:T(8,128)(2,1)S(1)} %get-tuple-element.28.rest_0_, f8e4m3fn[1536,512]{1,0:T(32,128)(4,1)S(1)} %get-tuple-element.29.rest_1_, f32[1536,128]{1,0:T(8,128)S(1)} %get-tuple-element.30.rest_2_, f32[1536,128]{1,0:T(8,128)S(1)} %get-tuple-element.38.rest_3_, ...), custom_call_target="tpu_custom_call" | custom-call | flops 393216 | bytes 393216 | tf_op jit(solution)/shard_map/middle/pallas_call | solution.py:227
  44.5 1.2 %collective-permute-done.10.rest_7_ = f32[1,264,256]{2,1,0:T(8,128)S(1)} collective-permute-done((f32[1,264,256]{2,1,0:T(8,128)S(1)}, f32[1,264,256]{2,1,0:T(8,128)S(1)}, u32[]{:S(2)}, u32[]{:S(2)}) %collective-permute-start.10) | collective-permute-done | bytes 270368 | tf_op jit(solution)/shard_map/ppermute | solution.py:283
  45.7 2.4 %collective-permute-done.11.rest_8_ = f32[1,264,256]{2,1,0:T(8,128)S(1)} collective-permute-done((f32[1,264,256]{2,1,0:T(8,128)S(1)}, f32[1,264,256]{2,1,0:T(8,128)S(1)}, u32[]{:S(2)}, u32[]{:S(2)}) %collective-permute-start.11) | collective-permute-done | bytes 270368 | tf_op jit(solution)/shard_map/ppermute | solution.py:283
  48.2 0.5 collective-permute-start.16
  48.7 1.0 %collective-permute-done.15.rest_9_ = f32[1,264,256]{2,1,0:T(8,128)S(1)} collective-permute-done((f32[1,264,256]{2,1,0:T(8,128)S(1)}, f32[1,264,256]{2,1,0:T(8,128)S(1)}, u32[]{:S(2)}, u32[]{:S(2)}) %collective-permute-start.15) | collective-permute-done | bytes 270368 | tf_op jit(solution)/shard_map/ppermute | solution.py:283
  50.1 13.3 %closing.1 = f32[16,8,1,512]{3,2,1,0:T(1,128)S(1)} custom-call(s32[16]{0:T(128)S(1)} %stack.67.place_ref, bf16[1536,256]{1,0:T(8,128)(2,1)} %copy-done, f8e4m3fn[1536,512]{1,0:T(32,128)(4,1)} %copy-done.1, f32[1536,128]{1,0:T(8,128)} %copy-done.2, f32[1536,128]{1,0:T(8,128)S(1)} %get-tuple-element.41.rest_3_, ...), custom_call_target="tpu_custom_call" | custom-call | flops 393216 | bytes 393216 | tf_op jit(solution)/shard_map/closing/pallas_call | solution.py:248
  63.5 18.8 %all_to_all.5 = f32[128,1,512]{2,1,0:T(1,128)S(1)} all-to-all(f32[128,1,512]{2,1,0:T(1,128)S(1)} %bitcast.19), channel_id=1, replica_groups=mesh['blk'=16,'rows'=8] {'blk','rows'}, dimensions={0} | all-to-all | bytes 524288 | tf_op jit(solution)/shard_map/all_to_all | solution.py:329
  82.5 0.6 broadcast_multiply_fusion
  (35 shorter events, 1.9 us)
Async XLA Ops:
  1.2 5.0 %collective-permute-start.3 = (f32[2,264,256]{2,1,0:T(8,128)S(1)}, f32[2,264,256]{2,1,0:T(8,128)S(1)}, u32[]{:S(2)}, u32[]{:S(2)}) collective-permute-start(f32[2,264,256]{2,1,0:T(8,128)S(1)} %maximum_maximum_fusion.rest_0_), channel_id=1, source_target_pairs={{8,0},{0,8},{24,16},{16,24},{40,32},{32,40},{56,48},{48,56},{72,64... | collective-permute-start | bytes 1622024 | tf_op jit(solution)/shard_map/ppermute | solution.py:283
  1.3 15.1 %collective-permute-start = (f32[2,264,256]{2,1,0:T(8,128)S(1)}, f32[2,264,256]{2,1,0:T(8,128)S(1)}, u32[]{:S(2)}, u32[]{:S(2)}) collective-permute-start(f32[2,264,256]{2,1,0:T(8,128)S(1)} %maximum_maximum_fusion.rest_0_), channel_id=1, source_target_pairs={{32,0},{40,8},{48,16},{56,24},{64,32},{72,40},{80,48},{88,56},{96,... | collective-permute-start | bytes 1622024 | tf_op jit(solution)/shard_map/ppermute | solution.py:283
  4.2 15.6 %collective-permute-start.1 = (f32[2,264,256]{2,1,0:T(8,128)S(1)}, f32[2,264,256]{2,1,0:T(8,128)S(1)}, u32[]{:S(2)}, u32[]{:S(2)}) collective-permute-start(f32[2,264,256]{2,1,0:T(8,128)S(1)} %maximum_maximum_fusion.rest_0_), channel_id=1, source_target_pairs={{96,0},{104,8},{112,16},{120,24},{0,32},{8,40},{16,48},{24,56},{32... | collective-permute-start | bytes 1622024 | tf_op jit(solution)/shard_map/ppermute | solution.py:283
  4.3 15.6 %collective-permute-start.2 = (f32[2,264,256]{2,1,0:T(8,128)S(1)}, f32[2,264,256]{2,1,0:T(8,128)S(1)}, u32[]{:S(2)}, u32[]{:S(2)}) collective-permute-start(f32[2,264,256]{2,1,0:T(8,128)S(1)} %maximum_maximum_fusion.rest_0_), channel_id=1, source_target_pairs={{16,0},{24,8},{0,16},{8,24},{48,32},{56,40},{32,48},{40,56},{80,64... | collective-permute-start | bytes 1622024 | tf_op jit(solution)/shard_map/ppermute | solution.py:283
  6.3 0.8 copy-start.4
  7.1 1.4 %copy-start.3 = (f32[1536,256]{1,0:T(8,128)S(1)}, f32[1536,256]{1,0:T(8,128)}, u32[]{:S(2)}) copy-start(f32[1536,256]{1,0:T(8,128)} %x_ref.1) | copy-start | bytes 4718596
  8.5 1.0 %copy-start.5 = (f32[2,264,256]{2,1,0:T(8,128)S(1)}, f32[2,264,256]{2,1,0:T(8,128)}, u32[]{:S(2)}) copy-start(f32[2,264,256]{2,1,0:T(8,128)} %copy-done.4) | copy-start | bytes 1622020
  12.7 37.4 %copy-start = (bf16[1536,256]{1,0:T(8,128)(2,1)}, bf16[1536,256]{1,0:T(8,128)(2,1)S(1)}, u32[]{:S(2)}) copy-start(bf16[1536,256]{1,0:T(8,128)(2,1)S(1)} %get-tuple-element.28.rest_0_) | copy-start | bytes 2359300
  12.7 37.4 %copy-start.1 = (f8e4m3fn[1536,512]{1,0:T(32,128)(4,1)}, f8e4m3fn[1536,512]{1,0:T(32,128)(4,1)S(1)}, u32[]{:S(2)}) copy-start(f8e4m3fn[1536,512]{1,0:T(32,128)(4,1)S(1)} %get-tuple-element.29.rest_1_) | copy-start | bytes 2359300
  12.7 37.4 %copy-start.2 = (f32[1536,128]{1,0:T(8,128)}, f32[1536,128]{1,0:T(8,128)S(1)}, u32[]{:S(2)}) copy-start(f32[1536,128]{1,0:T(8,128)S(1)} %get-tuple-element.30.rest_2_) | copy-start | bytes 2359300
  19.8 2.5 %collective-permute-start.7 = (f32[2,264,256]{2,1,0:T(8,128)S(1)}, f32[2,264,256]{2,1,0:T(8,128)S(1)}, u32[]{:S(2)}, u32[]{:S(2)}) collective-permute-start(f32[2,264,256]{2,1,0:T(8,128)S(1)} %collective-permute-done.rest_4_), channel_id=1, source_target_pairs={{8,0},{0,8},{24,16},{16,24},{40,32},{32,40},{56,48},{48,56},{72,64... | collective-permute-start | bytes 1622024 | tf_op jit(solution)/shard_map/ppermute | solution.py:283
  19.8 4.5 %collective-permute-start.8 = (f32[2,264,256]{2,1,0:T(8,128)S(1)}, f32[2,264,256]{2,1,0:T(8,128)S(1)}, u32[]{:S(2)}, u32[]{:S(2)}) collective-permute-start(f32[2,264,256]{2,1,0:T(8,128)S(1)} %collective-permute-done.1.rest_5_), channel_id=1, source_target_pairs={{8,0},{0,8},{24,16},{16,24},{40,32},{32,40},{56,48},{48,56},{72,64... | collective-permute-start | bytes 1622024 | tf_op jit(solution)/shard_map/ppermute | solution.py:283
  20.3 4.0 %collective-permute-start.9 = (f32[2,264,256]{2,1,0:T(8,128)S(1)}, f32[2,264,256]{2,1,0:T(8,128)S(1)}, u32[]{:S(2)}, u32[]{:S(2)}) collective-permute-start(f32[2,264,256]{2,1,0:T(8,128)S(1)} %collective-permute-done.2.rest_6_), channel_id=1, source_target_pairs={{8,0},{0,8},{24,16},{16,24},{40,32},{32,40},{56,48},{48,56},{72,64... | collective-permute-start | bytes 1622024 | tf_op jit(solution)/shard_map/ppermute | solution.py:283
  20.3 14.7 %collective-permute-start.4 = (f32[2,264,256]{2,1,0:T(8,128)S(1)}, f32[2,264,256]{2,1,0:T(8,128)S(1)}, u32[]{:S(2)}, u32[]{:S(2)}) collective-permute-start(f32[2,264,256]{2,1,0:T(8,128)S(1)} %collective-permute-done.rest_4_), channel_id=1, source_target_pairs={{32,0},{40,8},{48,16},{56,24},{64,32},{72,40},{80,48},{88,56},{96,... | collective-permute-start | bytes 1622024 | tf_op jit(solution)/shard_map/ppermute | solution.py:283
  22.2 15.6 %collective-permute-start.5 = (f32[2,264,256]{2,1,0:T(8,128)S(1)}, f32[2,264,256]{2,1,0:T(8,128)S(1)}, u32[]{:S(2)}, u32[]{:S(2)}) collective-permute-start(f32[2,264,256]{2,1,0:T(8,128)S(1)} %collective-permute-done.2.rest_6_), channel_id=1, source_target_pairs={{96,0},{104,8},{112,16},{120,24},{0,32},{8,40},{16,48},{24,56},{32... | collective-permute-start | bytes 1622024 | tf_op jit(solution)/shard_map/ppermute | solution.py:283
  22.4 15.5 %collective-permute-start.6 = (f32[2,264,256]{2,1,0:T(8,128)S(1)}, f32[2,264,256]{2,1,0:T(8,128)S(1)}, u32[]{:S(2)}, u32[]{:S(2)}) collective-permute-start(f32[2,264,256]{2,1,0:T(8,128)S(1)} %collective-permute-done.rest_4_), channel_id=1, source_target_pairs={{16,0},{24,8},{0,16},{8,24},{48,32},{56,40},{32,48},{40,56},{80,64... | collective-permute-start | bytes 1622024 | tf_op jit(solution)/shard_map/ppermute | solution.py:283
  37.9 7.9 %collective-permute-start.10 = (f32[1,264,256]{2,1,0:T(8,128)S(1)}, f32[1,264,256]{2,1,0:T(8,128)S(1)}, u32[]{:S(2)}, u32[]{:S(2)}) collective-permute-start(f32[1,264,256]{2,1,0:T(8,128)S(1)} %slice.6), channel_id=1, source_target_pairs={{32,0},{40,8},{48,16},{56,24},{64,32},{72,40},{80,48},{88,56},{96,... | collective-permute-start | bytes 811016 | tf_op jit(solution)/shard_map/ppermute | solution.py:283
  39.7 8.5 %collective-permute-start.11 = (f32[1,264,256]{2,1,0:T(8,128)S(1)}, f32[1,264,256]{2,1,0:T(8,128)S(1)}, u32[]{:S(2)}, u32[]{:S(2)}) collective-permute-start(f32[1,264,256]{2,1,0:T(8,128)S(1)} %slice.7), channel_id=1, source_target_pairs={{96,0},{104,8},{112,16},{120,24},{0,32},{8,40},{16,48},{24,56},{32... | collective-permute-start | bytes 811016 | tf_op jit(solution)/shard_map/ppermute | solution.py:283
  40.1 8.6 %collective-permute-start.12 = (f32[2,264,256]{2,1,0:T(8,128)S(1)}, f32[2,264,256]{2,1,0:T(8,128)S(1)}, u32[]{:S(2)}, u32[]{:S(2)}) collective-permute-start(f32[2,264,256]{2,1,0:T(8,128)S(1)} %collective-permute-done.4.rest_4_), channel_id=1, source_target_pairs={{8,0},{0,8},{24,16},{16,24},{40,32},{32,40},{56,48},{48,56},{72,64... | collective-permute-start | bytes 1622024 | tf_op jit(solution)/shard_map/ppermute | solution.py:283
  40.1 8.6 %collective-permute-start.13 = (f32[2,264,256]{2,1,0:T(8,128)S(1)}, f32[2,264,256]{2,1,0:T(8,128)S(1)}, u32[]{:S(2)}, u32[]{:S(2)}) collective-permute-start(f32[2,264,256]{2,1,0:T(8,128)S(1)} %collective-permute-done.5.rest_5_), channel_id=1, source_target_pairs={{8,0},{0,8},{24,16},{16,24},{40,32},{32,40},{56,48},{48,56},{72,64... | collective-permute-start | bytes 1622024 | tf_op jit(solution)/shard_map/ppermute | solution.py:283
  40.6 8.1 %collective-permute-start.14 = (f32[2,264,256]{2,1,0:T(8,128)S(1)}, f32[2,264,256]{2,1,0:T(8,128)S(1)}, u32[]{:S(2)}, u32[]{:S(2)}) collective-permute-start(f32[2,264,256]{2,1,0:T(8,128)S(1)} %collective-permute-done.6.rest_6_), channel_id=1, source_target_pairs={{8,0},{0,8},{24,16},{16,24},{40,32},{32,40},{56,48},{48,56},{72,64... | collective-permute-start | bytes 1622024 | tf_op jit(solution)/shard_map/ppermute | solution.py:283
  48.2 1.5 %collective-permute-start.15 = (f32[1,264,256]{2,1,0:T(8,128)S(1)}, f32[1,264,256]{2,1,0:T(8,128)S(1)}, u32[]{:S(2)}, u32[]{:S(2)}) collective-permute-start(f32[1,264,256]{2,1,0:T(8,128)S(1)} %collective-permute-done.10.rest_7_), channel_id=1, source_target_pairs={{8,0},{0,8},{24,16},{16,24},{40,32},{32,40},{56,48},{48,56},{72,64... | collective-permute-start | bytes 811016 | tf_op jit(solution)/shard_map/ppermute | solution.py:283
  48.2 1.9 %collective-permute-start.16 = (f32[1,264,256]{2,1,0:T(8,128)S(1)}, f32[1,264,256]{2,1,0:T(8,128)S(1)}, u32[]{:S(2)}, u32[]{:S(2)}) collective-permute-start(f32[1,264,256]{2,1,0:T(8,128)S(1)} %collective-permute-done.11.rest_8_), channel_id=1, source_target_pairs={{8,0},{0,8},{24,16},{16,24},{40,32},{32,40},{56,48},{48,56},{72,64... | collective-permute-start | bytes 811016 | tf_op jit(solution)/shard_map/ppermute | solution.py:283
